TPU v7x, 32 devices: a whole 2x2x4 slice. The times are simulated.
32 devices in a mesh: dp: 4 (over x, core), ctx: 8 (over z, y).
Axes of the slice: x: 2, y: 2, z: 4, core: 2. Of those that a mesh axis runs over, the one named last changes fastest.
Arguments:
- query_proj: bfloat16 [4, 1024, 4096], P('dp', 'ctx'), may hold values from -6 to 6
- key_proj: bfloat16 [4, 1024, 4096], P('dp', 'ctx'), may hold values from -6 to 6
- value_proj: bfloat16 [4, 1024, 4096], P('dp', 'ctx'), may hold values from -6 to 6
- doc_offset: int32 [4, 1024], P('dp', 'ctx'), may hold values from 0 to 1023, as said below
- short_taps: float32 [3, 7, 4096], replicated, may hold values from -2.5 to 2.5
- rate_scale: float32 [16, 4096], replicated, may hold values from 0.1 to 120
- residue: float32 [16, 4096], replicated, may hold values from -2.5 to 2.5
- skip_gain: float32 [4096], replicated, may hold values from 0.5 to 1.5
- out_grad: bfloat16 [4, 1024, 4096], P('dp', 'ctx'), may hold values from -6 to 6
Outputs:
- mixed_out: bfloat16 [4, 1024, 4096], P('dp', 'ctx')
- query_grad: bfloat16 [4, 1024, 4096], P('dp', 'ctx')
- key_grad: bfloat16 [4, 1024, 4096], P('dp', 'ctx')
- value_grad: bfloat16 [4, 1024, 4096], P('dp', 'ctx')
- taps_grad: float32 [3, 7, 4096], replicated
- skip_grad: float32 [4096], replicated
- residue_grad: float32 [16, 4096], replicated
Inputs may be any that keep to these rules, and one draw needn't show every extreme that they name: `doc_offset`: each row is a run of whole documents: the value is a token's index inside its document, 0 at a document's first position and rising by one along it. The first row holds a single document.
All inputs are finite; a program needn't handle non-finite values.
Results may differ from a plain program's by a relative error of at most 0.0013.
Values may be sent and summed in bfloat16 or wider, within the bound.
A program may use at most 192 MiB of HBM per device.

v0:
```python
import math

import jax
import jax.numpy as jnp
from jax import lax
from jax.sharding import PartitionSpec as P


def from_behind(block, axis, distance):
    devices = range(lax.axis_size(axis))
    route = [(i - distance, i) for i in devices if i - distance in devices]
    return lax.ppermute(block, axis, route)


def shards(
    query_proj,
    key_proj,
    value_proj,
    doc_offset,
    short_taps,
    rate_scale,
    residue,
    skip_gain,
    out_grad,
):
    row_count, tok_len, channels = query_proj.shape
    ctx_count = lax.axis_size("ctx")
    seq_len = tok_len * ctx_count
    total_tokens = row_count * lax.axis_size("dp") * seq_len
    ctx_index = lax.axis_index("ctx")
    tap_count = short_taps.shape[1]
    rim_len = tap_count - 1
    block_len = math.gcd(tok_len, 16)
    sub_count = tok_len // block_len
    rims = from_behind(
        (
            query_proj[:, tok_len - rim_len :, :],
            key_proj[:, tok_len - rim_len :, :],
            value_proj[:, tok_len - rim_len :, :],
        ),
        "ctx",
        1,
    )
    sources = (query_proj, key_proj, value_proj)
    extended = jnp.stack(
        [
            jnp.concatenate([rims[branch_index], sources[branch_index]], axis=1)
            for branch_index in range(3)
        ],
        axis=0,
    )
    tap_masks = [(doc_offset >= tap_index)[None, :, :, None] for tap_index in range(tap_count)]

    def window(tap_index):
        piece = extended[:, :, rim_len - tap_index : rim_len - tap_index + tok_len, :].astype(
            jnp.float32
        )
        return jnp.where(tap_masks[tap_index], piece, 0.0)

    shorts = jnp.zeros((3, row_count, tok_len, channels), jnp.float32)
    for tap_index in range(tap_count):
        shorts = shorts + short_taps[:, tap_index][:, None, None, :] * window(tap_index)
    query_short = shorts[0]
    key_short = shorts[1]
    value_short = shorts[2]
    lam_log = -rate_scale / seq_len
    decay_step = jnp.exp(lam_log)
    norm_factor = jnp.sqrt(-jnp.expm1(2.0 * lam_log))
    mode_coef = residue * norm_factor
    slot_index = jnp.arange(block_len, dtype=jnp.int32)
    slot_float = slot_index.astype(jnp.float32)
    pow_zero = jnp.exp(slot_float[:, None, None] * lam_log[None, :, :])
    pow_one = pow_zero * decay_step[None]
    pow_end = pow_zero[::-1]
    pow_back = pow_one[::-1]
    filter_taps = jnp.sum(mode_coef[None] * pow_zero, axis=1)
    decay_block = jnp.exp(block_len * lam_log)
    offsets = doc_offset.reshape(row_count, sub_count, block_len)
    valid_in = (offsets > slot_index[None, None, :]).astype(jnp.float32)[..., None]
    last_doc = (slot_index[None, None, :] >= block_len - 1 - offsets[:, :, -1:]).astype(
        jnp.float32
    )[..., None]
    pass_sub = (offsets[:, :, -1] >= block_len).astype(jnp.float32)
    pass_dev = (doc_offset[:, -1] >= tok_len).astype(jnp.float32)
    zero_state = jnp.zeros((row_count,) + rate_scale.shape, jnp.float32)
    lag_masks = [(offsets >= lag)[..., None] for lag in range(block_len)]

    def intra_backward(grads):
        total = jnp.zeros_like(grads)
        for lag in range(block_len):
            masked = jnp.where(lag_masks[lag], grads, 0.0)
            padded = jnp.pad(masked, ((0, 0), (0, 0), (0, block_len), (0, 0)))
            total = total + filter_taps[lag] * padded[:, :, lag : lag + block_len, :]
        return total

    def sweep(initial, terms, reverse_flag):

        def advance(carried, inputs):
            passed, term = inputs
            return (term + decay_block * passed[:, None, None] * carried, carried)

        return lax.scan(advance, initial, (pass_sub.T, terms), reverse=reverse_flag)

    mixed = key_short * value_short
    mixed_blocks = mixed.reshape(row_count, sub_count, block_len, channels)
    intra_padded = jnp.pad(mixed_blocks, ((0, 0), (0, 0), (block_len, 0), (0, 0)))
    total = jnp.zeros_like(mixed_blocks)
    for intra_lag in range(block_len):
        shifted = intra_padded[:, :, block_len - intra_lag : 2 * block_len - intra_lag, :]
        total = total + filter_taps[intra_lag] * jnp.where(lag_masks[intra_lag], shifted, 0.0)
    sigma = jnp.swapaxes(
        jnp.sum(pow_end[None, None] * (mixed_blocks * last_doc)[:, :, :, None, :], axis=2), 0, 1
    )
    block_sum, _ = sweep(zero_state, sigma, False)
    first_source = (ctx_index * tok_len - doc_offset[:, 0]) // tok_len
    sums = lax.all_gather(block_sum[None], "ctx", axis=0, tiled=True)
    marks = lax.all_gather(pass_dev[None], "ctx", axis=0, tiled=True)
    source = jnp.arange(sums.shape[0], dtype=jnp.int32)
    weight = jnp.logical_and(
        source[:, None] < ctx_index, source[:, None] >= first_source[None, :]
    ).astype(jnp.float32)
    distance = jnp.maximum(ctx_index - 1 - source, 0).astype(jnp.float32)
    decay_span = jnp.exp((tok_len * distance)[:, None, None] * lam_log[None])
    states = jnp.sum(weight[:, :, None, None] * decay_span[:, None] * sums, axis=0)
    _, enters = sweep(states, sigma, False)
    cross = valid_in * jnp.sum(
        (mode_coef[None] * pow_one)[None, None] * jnp.swapaxes(enters, 0, 1)[:, :, None], axis=3
    )
    long_out = (total + cross).reshape(row_count, tok_len, channels)
    z_full = long_out + skip_gain * mixed
    mixed_out = (query_short * z_full).astype(jnp.bfloat16)
    grad_in = out_grad.astype(jnp.float32)
    z_grad = grad_in * query_short
    query_short_grad = grad_in * z_full
    grad_blocks = z_grad.reshape(row_count, sub_count, block_len, channels)
    inner_back = intra_backward(grad_blocks)
    gamma = jnp.swapaxes(
        jnp.sum(pow_zero[None, None] * (grad_blocks * valid_in)[:, :, :, None, :], axis=2), 0, 1
    )
    block_adj, _ = sweep(zero_state, gamma, True)
    device_ids = jnp.arange(ctx_count, dtype=jnp.int32)
    blocked = jnp.logical_and(device_ids[:, None] > ctx_index, marks < 0.5)
    last_source = jnp.min(jnp.where(blocked, device_ids[:, None], ctx_count - 1), axis=0)
    piece = lax.all_gather(block_adj[None], "ctx", axis=0, tiled=True)
    source = jnp.arange(piece.shape[0], dtype=jnp.int32)
    weight = jnp.logical_and(
        source[:, None] > ctx_index, source[:, None] <= last_source[None, :]
    ).astype(jnp.float32)
    distance = jnp.maximum(source - ctx_index - 1, 0).astype(jnp.float32)
    decay_span = jnp.exp((tok_len * distance)[:, None, None] * lam_log[None])
    adj_in = jnp.sum(weight[:, :, None, None] * decay_span[:, None] * piece, axis=0)
    _, exits = sweep(adj_in, gamma, True)
    cross_back = last_doc * jnp.sum(
        (mode_coef[None] * pow_back)[None, None] * jnp.swapaxes(exits, 0, 1)[:, :, None], axis=3
    )
    mixed_grad = (inner_back + cross_back).reshape(
        row_count, tok_len, channels
    ) + skip_gain * z_grad
    key_short_grad = mixed_grad * value_short
    value_short_grad = mixed_grad * key_short
    padded_mixed = jnp.pad(mixed_blocks, ((0, 0), (0, 0), (block_len, 0), (0, 0)))
    lag_sums = jnp.stack(
        [
            jnp.sum(
                grad_blocks
                * jnp.where(
                    lag_masks[lag],
                    padded_mixed[:, :, block_len - lag : 2 * block_len - lag, :],
                    0.0,
                ),
                axis=(0, 1, 2),
            )
            for lag in range(block_len)
        ],
        axis=0,
    )
    residue_term = norm_factor * (
        jnp.sum(lag_sums[:, None, :] * pow_zero, axis=0)
        + jnp.sum(decay_step[None, None] * gamma * enters, axis=(0, 1))
    )
    skip_term = jnp.sum(z_grad * mixed, axis=(0, 1))
    short_grads = jnp.stack([query_short_grad, key_short_grad, value_short_grad], axis=0)
    spread = jnp.zeros((3, row_count, tok_len + rim_len, channels), jnp.float32)
    tap_terms = []
    for tap_index in range(tap_count):
        masked = jnp.where(tap_masks[tap_index], short_grads, 0.0)
        padded = jnp.pad(masked, ((0, 0), (0, 0), (rim_len, rim_len), (0, 0)))
        spread = (
            spread
            + short_taps[:, tap_index][:, None, None, :]
            * padded[:, :, tap_index : tap_index + tok_len + rim_len, :]
        )
        tap_terms.append(jnp.sum(window(tap_index) * short_grads, axis=(1, 2)))
    heads = spread[:, :, :rim_len, :]
    owns = spread[:, :, rim_len:, :]
    incoming = from_behind((heads[0], heads[1], heads[2]), "ctx", -1)
    input_grads = [
        (
            owns[branch_index]
            + jnp.pad(incoming[branch_index], ((0, 0), (tok_len - rim_len, 0), (0, 0)))
        ).astype(jnp.bfloat16)
        for branch_index in range(3)
    ]
    taps_sum, skip_sum, residue_sum = lax.psum(
        (jnp.stack(tap_terms, axis=1), skip_term, residue_term), ("dp", "ctx")
    )
    scale = 1.0 / math.sqrt(total_tokens)
    return (
        mixed_out,
        input_grads[0],
        input_grads[1],
        input_grads[2],
        taps_sum * scale,
        skip_sum * scale,
        residue_sum * scale,
    )


def solution(mesh):
    in_specs = (
        P("dp", "ctx", None),
        P("dp", "ctx", None),
        P("dp", "ctx", None),
        P("dp", "ctx"),
        P(),
        P(),
        P(),
        P(),
        P("dp", "ctx", None),
    )
    out_specs = (
        P("dp", "ctx", None),
        P("dp", "ctx", None),
        P("dp", "ctx", None),
        P("dp", "ctx", None),
        P(),
        P(),
        P(),
    )
    return jax.shard_map(shards, mesh=mesh, in_specs=in_specs, out_specs=out_specs, check_vma=False)
```

profile of v0, /device:TPU:0, one launch (start us, length us, event | category | flops | bytes accessed | tf_op | source)
XLA Modules:
  0.0 597.5 jit_solution(7358654868621144098)
XLA Ops:
  8.2 4.9 collective-permute-start.2
  14.0 3.4 collective-permute-start.1
  18.9 3.4 collective-permute-start
  32.7 18.6 %all-reduce.26 = f32[8]{0:T(128)S(1)} all-reduce(f32[8]{0:T(128)S(1)} %bitcast_dynamic-update-slice_fusion.9), channel_id=1, replica_groups=mesh['dp'=4,'ctx'=8] {'ctx'}, use_global_device_ids=true, to_apply=%add.26 | all-reduce | flops 8 | bytes 64
  53.2 2.9 fusion.83
  62.3 9.3 %multiply_add_fusion = f32[3,1,128,4096]{3,2,1,0:T(8,128)S(1)} fusion(f32[3,4096]{1,0:T(4,128)S(1)} %copy-done.29, f32[3,4096]{1,0:T(4,128)S(1)} %copy-done.31, f32[3,4096]{1,0:T(4,128)S(1)} %get-tuple-element.545, f32[3,4096]{1,0:T(4,128)S(1)} %get-tuple-element.546, f32[3,4096]{1,0:T(4,128)S(1)} %get-tuple-element.547, f32[3,4096]{1,0:T(4,128)S(1)} %copy-done.27, ...), kind=kLoop, calls=%fused_computation.61 | loop fusion | flops 42467328 | bytes 28656512 | tf_op jit(solution)/shard_map/add | solution.py:62
  75.6 2.6 multiply_reduce_fusion.28
  78.4 4.1 multiply_reduce_fusion.22
  82.6 4.7 multiply_reduce_fusion.13
  87.3 3.3 stack.131
  90.6 8.0 %fusion.17 = (f32[16,16,4096]{2,1,0:T(8,128)}, f32[16,16,4096]{2,1,0:T(8,128)}, f32[16,4096]{1,0:T(8,128)}, f32[16,4096]{1,0:T(8,128)}, f32[16,16,4096]{2,1,0:T(8,128)}) fusion(f32[16,4096]{1,0:T(8,128)} %get-tuple-element.513, f32[16,4096]{1,0:T(8,128)} %get-tuple-element.514, f32[16]{0:T(128)} %iota_convert_fusion, f32[16,4096]{1,0:T(8,128)} %get-tuple-element.516, ...), kind=kLoop, calls=%fused_computation.88 | loop fusion | flops 7208960 | bytes 14155840 | tf_op jit(solution)/shard_map/mul | solution.py:73
  98.6 4.7 rev.6
  106.2 4.0 multiply_reduce_fusion.1
  110.2 24.6 %while.57 = (s32[]{:T(128)}, f32[1,16,4096]{2,1,0:T(8,128)}, f32[8,1,16,4096]{3,2,1,0:T(8,128)}, f32[8,1]{0,1:T(1,128)S(1)}, f32[16,4096]{1,0:T(8,128)}, /*index=5*/s32[]{:T(128)}, s32[]{:T(128)}, s32[]{:T(128)}) while((s32[]{:T(128)}, f32[1,16,4096]{2,1,0:T(8,128)}, f32[8,1,16,4096]{3,2,1,0:T(8,128)}, f32[8,1]{0,1:T(1,128)S(1)}, ...), condition=%wide.region_11.12_spmd.clone, body=%wide.region_10.11_spmd.clone.sunk | while | flops 262148 | bytes 1048711 | solution.py:102
  113.8 2.5 fusion.93
  116.9 2.5 fusion.93
  119.9 2.5 fusion.93
  137.7 4.0 multiply_reduce_fusion.3
  141.7 29.5 %while.56 = (s32[]{:T(128)}, f32[1,16,4096]{2,1,0:T(8,128)}, f32[8,1,16,4096]{3,2,1,0:T(8,128)}, f32[8,1]{0,1:T(1,128)}, f32[16,4096]{1,0:T(8,128)}, /*index=5*/s32[]{:T(128)}, s32[]{:T(128)}) while((s32[]{:T(128)}, f32[1,16,4096]{2,1,0:T(8,128)}, f32[8,1,16,4096]{3,2,1,0:T(8,128)}, f32[8,1]{0,1:T(1,128)}, f32[16,4096]{1,0:T(8,128)}, ...), condition=%wide.region_3.4_spmd.clone, body=%wide.region_2.3_spmd.clone.sunk | while | flops 262147 | bytes 1048691 | solution.py:102
  146.5 2.5 fusion.92
  150.2 2.5 fusion.92
  153.8 2.5 fusion.92
  157.5 2.7 fusion.92
  161.4 2.5 fusion.92
  165.0 2.5 fusion.92
  168.7 2.5 fusion.92
  171.2 36.9 %psum.22 = f32[4096]{0:T(1024)} all-reduce(f32[4096]{0:T(1024)S(1)} %copy-done.51), channel_id=1, replica_groups=mesh['dp'=4,'ctx'=8] {'dp','ctx'}, use_global_device_ids=true, to_apply=%region_25.26 | all-reduce | flops 4096 | bytes 32768 | tf_op jit(solution)/shard_map/psum | solution.py:204
  209.5 2.7 fusion.84
  212.4 4.9 reverse_multiply_fusion
  217.4 10.3 %broadcast_select_fusion.8 = (f32[1,8,16,4096]{3,2,1,0:T(8,128)}, f32[1,8,16,4096]{3,2,1,0:T(8,128)}, f32[1,8,16,4096]{3,2,1,0:T(8,128)}, f32[1,8,16,4096]{3,2,1...) fusion(pred[8,16]{1,0:T(8,128)(4,1)S(1)} %copy-done.56, ...), kind=kLoop, calls=%fused_computation.199 | loop fusion | flops 7340032 | bytes 31459072 | tf_op jit(solution)/shard_map/jit(_where)/select_n | solution.py:91
  227.7 31.7 %all-gather.5.cloned.1.call-done = f32[8,16,4096]{2,1,0:T(8,128)} async-done(((f32[1,16,4096]{2,1,0:T(8,128)}), f32[8,16,4096]{2,1,0:T(8,128)}) %all-gather.5.cloned.1.call-update) | async-done | bytes 2097168 | tf_op jit(solution)/shard_map/all_gather | solution.py:116
  259.4 4.1 fusion.72
  265.1 42.7 %while.54 = (s32[]{:T(128)}, f32[1,16,4096]{2,1,0:T(8,128)}, f32[8,1,16,4096]{3,2,1,0:T(8,128)}, f32[8,1,16,4096]{3,2,1,0:T(8,128)}, f32[8,1]{0,1:T(1,128)}, /*index=5*/f32[16,4096]{1,0:T(8,128)}, s32[]{:T(128)}) while((s32[]{:T(128)}, f32[1,16,4096]{2,1,0:T(8,128)}, f32[8,1,16,4096]{3,2,1,0:T(8,128)}, f32[8,1,16,4096]{3,2,1,0:T(8,128)}, ...), condition=%wide.region_6.7_spmd, body=%wide.region_5.6_spmd.sunk | while | flops 196610 | bytes 1572973 | solution.py:102
  307.8 3.3 fusion.71
  312.6 42.8 %while.55 = (s32[]{:T(128)}, f32[1,16,4096]{2,1,0:T(8,128)}, f32[8,1,16,4096]{3,2,1,0:T(8,128)}, f32[8,1,16,4096]{3,2,1,0:T(8,128)}, f32[8,1]{0,1:T(1,128)}, /*index=5*/f32[16,4096]{1,0:T(8,128)}, s32[]{:T(128)}, s32[]{:T(128)}) while((s32[]{:T(128)}, f32[1,16,4096]{2,1,0:T(8,128)}, f32[8,1,16,4096]{3,2,1,0:T(8,128)}, ...), condition=%wide.region_14.15_spmd, body=%wide.region_13.14_spmd.sunk | while | flops 196611 | bytes 1572985 | solution.py:102
  355.4 9.7 %multiply_reduce_fusion.2 = f32[8,16,4096]{2,1,0:T(8,128)S(1)} fusion(f32[8,16,4096]{2,1,0:T(8,128)} %bitcast.280, f32[16,16,4096]{2,1,0:T(8,128)} %get-tuple-element.486), kind=kLoop, calls=%fused_computation.16 | loop fusion | flops 16252928 | bytes 8388608 | tf_op jit(solution)/shard_map/reduce_sum | solution.py:126
  365.2 9.6 %multiply_reduce_fusion = f32[8,16,4096]{2,1,0:T(8,128)S(1)} fusion(f32[8,16,4096]{2,1,0:T(8,128)} %bitcast.282, f32[16,16,4096]{2,1,0:T(8,128)S(1)} %copy-done.9), kind=kLoop, calls=%fused_computation.14 | loop fusion | flops 16252928 | bytes 8388608 | tf_op jit(solution)/shard_map/reduce_sum | solution.py:153
  375.0 8.3 %fusion.75 = f32[1,8,16,4096]{3,2,1,0:T(8,128)} fusion(f32[8,16,4096]{2,1,0:T(8,128)S(1)} %multiply_reduce_fusion.2, f32[1,8,16,4096]{3,2,1,0:T(8,128)S(1)} %bitcast.275, f32[8,16]{1,0:T(8,128)} %get-tuple-element.518, f32[4096]{0:T(1024)S(1)} %bitcast.287, f32[4096]{0:T(1024)S(1)} %bitcast.289, f32[4096]{0:T(1024)S(1)} %bitcast.291, ...), kind=kLoop, calls=%fused_computation.170 | loop fusion | flops 25690112 | bytes 6556160 | tf_op jit(solution)/shard_map/add | solution.py:129
  383.5 7.9 %fusion.35 = f32[1,8,16,4096]{3,2,1,0:T(8,128)} fusion(f32[1,8,16,4096]{3,2,1,0:T(8,128)} %get-tuple-element.484, f32[1,8,16,4096]{3,2,1,0:T(8,128)S(1)} %copy-done.12, f32[1,8,16,4096]{3,2,1,0:T(8,128)S(1)} %copy-done.13, f32[1,8,16,4096]{3,2,1,0:T(8,128)S(1)} %copy-done.14, f32[1,8,16,4096]{3,2,1,0:T(8,128)S(1)} %copy-done.15, ...), kind=kLoop, calls=%fused_computation.116 | loop fusion | flops 17825792 | bytes 38011520 | tf_op jit(solution)/shard_map/add | solution.py:156
  391.5 8.2 %fusion.73 = (f32[1,1,128,4096]{3,2,1,0:T(8,128)S(1)}, f32[1,1,128,4096]{3,2,1,0:T(8,128)S(1)}, bf16[1,128,4096]{2,1,0:T(8,128)(2,1)}, f32[1,1,128,4096]{3,2,1,0:T(8,128)}) fusion(f32[3,1,128,4096]{3,2,1,0:T(8,128)} %copy-done.3, f32[1,128,4096]{2,1,0:T(8,128)S(1)} %copy-done.2, f32[4096]{0:T(1024)} %param.24, f32[1,8,16,4096]{3,2,1,0:T(8,128)} %fusion.35, ...), kind=kLoop, calls=%fused_computation.165 | loop fusion | flops 5242880 | bytes 23085056 | tf_op jit(solution)/shard_map/stack | solution.py:182
  399.8 11.4 %multiply_reduce_fusion.4 = (f32[3,4096]{1,0:T(4,128)S(1)}, f32[3,4096]{1,0:T(4,128)S(1)}, f32[3,4096]{1,0:T(4,128)S(1)}, f32[3,4096]{1,0:T(4,128)S(1)}, f32[3,4096]{1,0:T(4,128)S(1)}, /*index=5*/f32[3,4096]{1,0:T(4,128)S(1)}) fusion(pred[128]{0:T(512)(128)(4,1)S(1)} %copy-done.92, bf16[3,1,134,4096]{3,2,1,0:T(8,128)(2,1)S(1)} %pad_maximum_fusion.1, ...), kind=kLoop, calls=%fused_computation.54 | loop fusion | flops 40820736 | bytes 25461504 | tf_op jit(solution)/shard_map/reduce_sum | solution.py:193
  411.2 8.0 %multiply_reduce_fusion.10 = (f32[3,4096]{1,0:T(4,128)S(1)}, f32[3,1,128,4096]{3,2,1,0:T(8,128)}, f32[3,1,128,4096]{3,2,1,0:T(8,128)}, f32[3,1,128,4096]{3,2,1,0:T(8,128)}) fusion(pred[128]{0:T(512)(128)(4,1)S(1)} %copy-done.90, bf16[3,1,134,4096]{3,2,1,0:T(8,128)(2,1)S(1)} %pad_maximum_fusion.1, f32[1,1,128,4096]{3,2,1,0:T(8,128)S(1)} %get-tuple-element.451, ...), kind=kLoop, calls=%fused_computation.60 | loop fusion | flops 14143488 | bytes 28361088 | tf_op jit(solution)/shard_map/reduce_sum | solution.py:193
  419.3 9.9 %broadcast_select_fusion.2 = (f32[3,1,128,4096]{3,2,1,0:T(8,128)}, f32[3,1,128,4096]{3,2,1,0:T(8,128)}, f32[3,1,128,4096]{3,2,1,0:T(8,128)}, f32[3,1,128,4096]{3,2,1,0:T(8,128)}) fusion(pred[128]{0:T(512)(128)(4,1)S(1)} %copy-done.96, f32[1,1,128,4096]{3,2,1,0:T(8,128)S(1)} %get-tuple-element.451, f32[1,1,128,4096]{3,2,1,0:T(8,128)S(1)} %get-tuple-element.450, ...), kind=kLoop, calls=%fused_computation.92 | loop fusion | flops 9437184 | bytes 31457792 | tf_op jit(solution)/shard_map/jit(_where)/select_n | solution.py:186
  429.3 15.8 %fusion.10 = f32[3,1,134,4096]{3,2,1,0:T(8,128)S(1)} fusion(f32[3,1,128,4096]{3,2,1,0:T(8,128)} %get-tuple-element.463, f32[3,1,128,4096]{3,2,1,0:T(8,128)} %get-tuple-element.469, f32[3,1,128,4096]{3,2,1,0:T(8,128)} %get-tuple-element.468, f32[3,1,128,4096]{3,2,1,0:T(8,128)} %get-tuple-element.467, f32[3,1,128,4096]{3,2,1,0:T(8,128)} %get-tuple-element.466, ...), kind=kLoop, calls=%fused_computation.46 | loop fusion | flops 21405696 | bytes 50970624 | tf_op jit(solution)/shard_map/add | solution.py:189
  445.2 2.8 copy-done.8
  453.7 2.5 collective-permute-done.5
  460.1 5.0 fusion.66
  465.1 121.6 %all-reduce.30.cloned.1.call-done = (f32[3,7,4096]{2,0,1:T(4,128)}, f32[16,4096]{1,0:T(8,128)}) async-done(((f32[3,7,4096]{2,0,1:T(4,128)}, f32[16,4096]{1,0:T(8,128)}), (f32[3,7,4096]{2,0,1:T(4,128)}, f32[16,4096]{1,0:T(8,128)})) %all-reduce.30.cloned.1.call-update) | async-done | bytes 606224 | tf_op jit(solution)/shard_map/psum | solution.py:204
  (342 shorter events, 162.5 us)
Async XLA Ops:
  7.2 52.7 %copy-start.19 = (bf16[1,128,4096]{2,1,0:T(8,128)(2,1)S(1)}, bf16[1,128,4096]{2,1,0:T(8,128)(2,1)}, u32[]{:S(2)}) copy-start(bf16[1,128,4096]{2,1,0:T(8,128)(2,1)} %param.17) | copy-start | bytes 3145732
  7.2 51.1 %copy-start.24 = (f32[16,4096]{1,0:T(8,128)S(1)}, f32[16,4096]{1,0:T(8,128)}, u32[]{:S(2)}) copy-start(f32[16,4096]{1,0:T(8,128)} %param.22) | copy-start | bytes 786436
  7.2 51.1 %copy-start.35 = (f32[16,4096]{1,0:T(8,128)S(1)}, f32[16,4096]{1,0:T(8,128)}, u32[]{:S(2)}) copy-start(f32[16,4096]{1,0:T(8,128)} %param.23) | copy-start | bytes 786436
  7.2 220.5 %all-gather.7.cloned.1.call-start = ((), (), s32[]{:S(2)}) async-start(), calls=%async_computation.1 | async-start | bytes 2359296 | tf_op jit(solution)/shard_map/all_gather | solution.py:144
  8.2 52.3 %collective-permute-start.2 = (bf16[1,6,4096]{2,1,0:T(8,128)(2,1)S(1)}, bf16[1,6,4096]{2,1,0:T(8,128)(2,1)S(1)}, u32[]{:S(2)}, u32[]{:S(2)}) collective-permute-start(bf16[1,6,4096]{2,1,0:T(8,128)(2,1)S(1)} %slice.306), channel_id=1, source_target_pairs={{0,1},{1,2},{2,3},{3,4},{4,5},{5,6},{6,7},{8,9},{9,10},{10,11},{11... | collective-permute-start | bytes 147464 | tf_op jit(solution)/shard_map/ppermute | solution.py:12
  14.0 46.2 %collective-permute-start.1 = (bf16[1,6,4096]{2,1,0:T(8,128)(2,1)S(1)}, bf16[1,6,4096]{2,1,0:T(8,128)(2,1)S(1)}, u32[]{:S(2)}, u32[]{:S(2)}) collective-permute-start(bf16[1,6,4096]{2,1,0:T(8,128)(2,1)S(1)} %slice.305), channel_id=1, source_target_pairs={{0,1},{1,2},{2,3},{3,4},{4,5},{5,6},{6,7},{8,9},{9,10},{10,11},{11... | collective-permute-start | bytes 147464 | tf_op jit(solution)/shard_map/ppermute | solution.py:12
  18.9 41.0 %collective-permute-start = (bf16[1,6,4096]{2,1,0:T(8,128)(2,1)}, bf16[1,6,4096]{2,1,0:T(8,128)(2,1)S(1)}, u32[]{:S(2)}, u32[]{:S(2)}) collective-permute-start(bf16[1,6,4096]{2,1,0:T(8,128)(2,1)} %slice.304), channel_id=1, source_target_pairs={{0,1},{1,2},{2,3},{3,4},{4,5},{5,6},{6,7},{8,9},{9,10},{10,11},{11... | collective-permute-start | bytes 147464 | tf_op jit(solution)/shard_map/ppermute | solution.py:12
  26.1 35.8 %copy-start.88 = (pred[128]{0:T(512)(128)(4,1)}, pred[128]{0:T(512)(128)(4,1)S(1)}, u32[]{:S(2)}) copy-start(pred[128]{0:T(512)(128)(4,1)S(1)} %get-tuple-element.536) | copy-start | bytes 388
  26.1 35.8 %copy-start.91 = (pred[128]{0:T(512)(128)(4,1)}, pred[128]{0:T(512)(128)(4,1)S(1)}, u32[]{:S(2)}) copy-start(pred[128]{0:T(512)(128)(4,1)S(1)} %get-tuple-element.537) | copy-start | bytes 388
  26.1 35.8 %copy-start.93 = (pred[128]{0:T(512)(128)(4,1)}, pred[128]{0:T(512)(128)(4,1)S(1)}, u32[]{:S(2)}) copy-start(pred[128]{0:T(512)(128)(4,1)S(1)} %get-tuple-element.538) | copy-start | bytes 388
  56.8 15.2 %copy-start.85 = (pred[8,16]{1,0:T(8,128)(4,1)}, pred[8,16]{1,0:T(8,128)(4,1)S(1)}, u32[]{:S(2)}) copy-start(pred[8,16]{1,0:T(8,128)(4,1)S(1)} %get-tuple-element.519) | copy-start | bytes 388
  71.9 10.6 %copy-start.4 = (f32[1,1,128,4096]{3,2,1,0:T(8,128)}, f32[1,1,128,4096]{3,2,1,0:T(8,128)S(1)}, u32[]{:S(2)}) copy-start(f32[1,1,128,4096]{3,2,1,0:T(8,128)S(1)} %slice_multiply_fusion) | copy-start | bytes 6291460
  110.2 24.7 %copy-start.52 = (f32[8,16]{1,0:T(8,128)S(1)}, f32[8,16]{1,0:T(8,128)}, u32[]{:S(2)}) copy-start(f32[8,16]{1,0:T(8,128)} %get-tuple-element.551) | copy-start | bytes 1540
  134.8 124.6 %all-gather.5.cloned.1.call-start = ((), (), s32[]{:S(2)}) async-start(), calls=%async_computation | async-start | bytes 2359296 | tf_op jit(solution)/shard_map/all_gather | solution.py:116
  141.7 29.5 %copy-start.51 = (f32[4096]{0:T(1024)S(1)}, f32[4096]{0:T(1024)}, u32[]{:S(2)}) copy-start(f32[4096]{0:T(1024)} %get-tuple-element.396) | copy-start | bytes 49156
  208.2 378.6 %all-reduce.30.cloned.1.call-start = ((), (), s32[]{:S(2)}) async-start(), calls=%async_computation.2 | async-start | bytes 1441792 | tf_op jit(solution)/shard_map/psum | solution.py:204
  355.4 9.7 %copy-start.9 = (f32[16,16,4096]{2,1,0:T(8,128)S(1)}, f32[16,16,4096]{2,1,0:T(8,128)}, u32[]{:S(2)}) copy-start(f32[16,16,4096]{2,1,0:T(8,128)} %reverse_multiply_fusion) | copy-start | bytes 12582916
  355.4 19.4 %copy-start.39 = (f32[1,4096]{1,0:T(1,128)S(1)}, f32[1,4096]{1,0:T(1,128)}, u32[]{:S(2)}) copy-start(f32[1,4096]{1,0:T(1,128)} %get-tuple-element.501) | copy-start | bytes 49156
  355.4 27.9 %copy-start.16 = (f32[1,8,16,4096]{3,2,1,0:T(8,128)S(1)}, f32[1,8,16,4096]{3,2,1,0:T(8,128)}, u32[]{:S(2)}) copy-start(f32[1,8,16,4096]{3,2,1,0:T(8,128)} %get-tuple-element.476) | copy-start | bytes 6291460
  355.4 27.9 %copy-start.17 = (f32[1,8,16,4096]{3,2,1,0:T(8,128)S(1)}, f32[1,8,16,4096]{3,2,1,0:T(8,128)}, u32[]{:S(2)}) copy-start(f32[1,8,16,4096]{3,2,1,0:T(8,128)} %get-tuple-element.477) | copy-start | bytes 6291460
  365.1 9.7 %copy-start.5 = (f32[1,1,128,4096]{3,2,1,0:T(8,128)S(1)}, f32[1,1,128,4096]{3,2,1,0:T(8,128)}, u32[]{:S(2)}) copy-start(f32[1,1,128,4096]{3,2,1,0:T(8,128)} %copy-done.4) | copy-start | bytes 6291460
  365.1 9.7 %copy-start.36 = (f32[1,4096]{1,0:T(1,128)S(1)}, f32[1,4096]{1,0:T(1,128)}, u32[]{:S(2)}) copy-start(f32[1,4096]{1,0:T(1,128)} %get-tuple-element.498) | copy-start | bytes 49156
  365.1 9.7 %copy-start.37 = (f32[1,4096]{1,0:T(1,128)S(1)}, f32[1,4096]{1,0:T(1,128)}, u32[]{:S(2)}) copy-start(f32[1,4096]{1,0:T(1,128)} %get-tuple-element.499) | copy-start | bytes 49156
  365.1 9.7 %copy-start.38 = (f32[1,4096]{1,0:T(1,128)S(1)}, f32[1,4096]{1,0:T(1,128)}, u32[]{:S(2)}) copy-start(f32[1,4096]{1,0:T(1,128)} %get-tuple-element.500) | copy-start | bytes 49156
  365.2 9.7 %copy-start.57 = (pred[8,16]{1,0:T(8,128)(4,1)S(1)}, pred[8,16]{1,0:T(8,128)(4,1)}, u32[]{:S(2)}) copy-start(pred[8,16]{1,0:T(8,128)(4,1)} %get-tuple-element.520) | copy-start | bytes 388
  365.2 9.7 %copy-start.60 = (pred[8,16]{1,0:T(8,128)(4,1)S(1)}, pred[8,16]{1,0:T(8,128)(4,1)}, u32[]{:S(2)}) copy-start(pred[8,16]{1,0:T(8,128)(4,1)} %get-tuple-element.521) | copy-start | bytes 388
  365.2 18.2 %copy-start.13 = (f32[1,8,16,4096]{3,2,1,0:T(8,128)S(1)}, f32[1,8,16,4096]{3,2,1,0:T(8,128)}, u32[]{:S(2)}) copy-start(f32[1,8,16,4096]{3,2,1,0:T(8,128)} %get-tuple-element.473) | copy-start | bytes 6291460
  365.2 18.2 %copy-start.14 = (f32[1,8,16,4096]{3,2,1,0:T(8,128)S(1)}, f32[1,8,16,4096]{3,2,1,0:T(8,128)}, u32[]{:S(2)}) copy-start(f32[1,8,16,4096]{3,2,1,0:T(8,128)} %get-tuple-element.474) | copy-start | bytes 6291460
  365.2 18.2 %copy-start.15 = (f32[1,8,16,4096]{3,2,1,0:T(8,128)S(1)}, f32[1,8,16,4096]{3,2,1,0:T(8,128)}, u32[]{:S(2)}) copy-start(f32[1,8,16,4096]{3,2,1,0:T(8,128)} %get-tuple-element.475) | copy-start | bytes 6291460
  374.9 8.5 %copy-start.2 = (f32[1,128,4096]{2,1,0:T(8,128)S(1)}, f32[1,128,4096]{2,1,0:T(8,128)}, u32[]{:S(2)}) copy-start(f32[1,128,4096]{2,1,0:T(8,128)} %copy-done) | copy-start | bytes 6291460
  374.9 8.5 %copy-start.11 = (f32[1,8,16,4096]{3,2,1,0:T(8,128)S(1)}, f32[1,8,16,4096]{3,2,1,0:T(8,128)}, u32[]{:S(2)}) copy-start(f32[1,8,16,4096]{3,2,1,0:T(8,128)} %get-tuple-element.471) | copy-start | bytes 6291460
  374.9 8.5 %copy-start.12 = (f32[1,8,16,4096]{3,2,1,0:T(8,128)S(1)}, f32[1,8,16,4096]{3,2,1,0:T(8,128)}, u32[]{:S(2)}) copy-start(f32[1,8,16,4096]{3,2,1,0:T(8,128)} %get-tuple-element.472) | copy-start | bytes 6291460
  374.9 8.5 %copy-start.40 = (f32[1,4096]{1,0:T(1,128)S(1)}, f32[1,4096]{1,0:T(1,128)}, u32[]{:S(2)}) copy-start(f32[1,4096]{1,0:T(1,128)} %get-tuple-element.502) | copy-start | bytes 49156
  374.9 8.5 %copy-start.41 = (f32[1,4096]{1,0:T(1,128)S(1)}, f32[1,4096]{1,0:T(1,128)}, u32[]{:S(2)}) copy-start(f32[1,4096]{1,0:T(1,128)} %get-tuple-element.503) | copy-start | bytes 49156
  374.9 8.5 %copy-start.42 = (f32[1,4096]{1,0:T(1,128)S(1)}, f32[1,4096]{1,0:T(1,128)}, u32[]{:S(2)}) copy-start(f32[1,4096]{1,0:T(1,128)} %get-tuple-element.504) | copy-start | bytes 49156
  374.9 8.5 %copy-start.43 = (f32[1,4096]{1,0:T(1,128)S(1)}, f32[1,4096]{1,0:T(1,128)}, u32[]{:S(2)}) copy-start(f32[1,4096]{1,0:T(1,128)} %get-tuple-element.505) | copy-start | bytes 49156
  399.8 11.5 %copy-start.7 = (f32[1,1,128,4096]{3,2,1,0:T(8,128)S(1)}, f32[1,1,128,4096]{3,2,1,0:T(8,128)}, u32[]{:S(2)}) copy-start(f32[1,1,128,4096]{3,2,1,0:T(8,128)} %get-tuple-element.470) | copy-start | bytes 6291460
  399.8 11.5 %copy-start.90 = (pred[128]{0:T(512)(128)(4,1)S(1)}, pred[128]{0:T(512)(128)(4,1)}, u32[]{:S(2)}) copy-start(pred[128]{0:T(512)(128)(4,1)} %copy-done.88) | copy-start | bytes 388
  419.3 10.0 %copy-start.28 = (f32[3,4096]{1,0:T(4,128)S(1)}, f32[3,4096]{1,0:T(4,128)}, u32[]{:S(2)}) copy-start(f32[3,4096]{1,0:T(4,128)} %get-tuple-element.548) | copy-start | bytes 147460
  419.3 10.0 %copy-start.30 = (f32[3,4096]{1,0:T(4,128)S(1)}, f32[3,4096]{1,0:T(4,128)}, u32[]{:S(2)}) copy-start(f32[3,4096]{1,0:T(4,128)} %get-tuple-element.543) | copy-start | bytes 147460
  419.3 10.0 %copy-start.32 = (f32[3,4096]{1,0:T(4,128)S(1)}, f32[3,4096]{1,0:T(4,128)}, u32[]{:S(2)}) copy-start(f32[3,4096]{1,0:T(4,128)} %get-tuple-element.544) | copy-start | bytes 147460
  419.3 10.0 %copy-start.34 = (f32[3,1,4096]{2,0,1:T(4,128)S(1)}, f32[3,1,4096]{2,0,1:T(4,128)}, u32[]{:S(2)}) copy-start(f32[3,1,4096]{2,0,1:T(4,128)} %copy-done.33) | copy-start | bytes 147460
  429.3 22.6 %copy-start.22 = (f32[16,4096]{1,0:T(8,128)S(1)}, f32[16,4096]{1,0:T(8,128)}, u32[]{:S(2)}) copy-start(f32[16,4096]{1,0:T(8,128)} %get-tuple-element.488) | copy-start | bytes 786436
  429.3 22.6 %copy-start.23 = (f32[16,4096]{1,0:T(8,128)S(1)}, f32[16,4096]{1,0:T(8,128)}, u32[]{:S(2)}) copy-start(f32[16,4096]{1,0:T(8,128)} %fusion.71) | copy-start | bytes 786436
  429.3 22.6 %copy-start.25 = (f32[16,4096]{1,0:T(8,128)S(1)}, f32[16,4096]{1,0:T(8,128)}, u32[]{:S(2)}) copy-start(f32[16,4096]{1,0:T(8,128)} %param.22) | copy-start | bytes 786436
  448.0 8.3 %collective-permute-start.5 = (f32[1,6,4096]{2,1,0:T(8,128)S(1)}, f32[1,6,4096]{2,1,0:T(8,128)S(1)}, u32[]{:S(2)}, u32[]{:S(2)}) collective-permute-start(f32[1,6,4096]{2,1,0:T(8,128)S(1)} %get-tuple-element.458), channel_id=1, source_target_pairs={{1,0},{2,1},{3,2},{4,3},{5,4},{6,5},{7,6},{9,8},{10,9},{11,10},{12... | collective-permute-start | bytes 294920 | tf_op jit(solution)/shard_map/ppermute | solution.py:12
  449.3 9.5 %collective-permute-start.4 = (f32[1,6,4096]{2,1,0:T(8,128)S(1)}, f32[1,6,4096]{2,1,0:T(8,128)S(1)}, u32[]{:S(2)}, u32[]{:S(2)}) collective-permute-start(f32[1,6,4096]{2,1,0:T(8,128)S(1)} %get-tuple-element.459), channel_id=1, source_target_pairs={{1,0},{2,1},{3,2},{4,3},{5,4},{6,5},{7,6},{9,8},{10,9},{11,10},{12... | collective-permute-start | bytes 294920 | tf_op jit(solution)/shard_map/ppermute | solution.py:12
  450.6 9.6 %collective-permute-start.3 = (f32[1,6,4096]{2,1,0:T(8,128)S(1)}, f32[1,6,4096]{2,1,0:T(8,128)S(1)}, u32[]{:S(2)}, u32[]{:S(2)}) collective-permute-start(f32[1,6,4096]{2,1,0:T(8,128)S(1)} %get-tuple-element.460), channel_id=1, source_target_pairs={{1,0},{2,1},{3,2},{4,3},{5,4},{6,5},{7,6},{9,8},{10,9},{11,10},{12... | collective-permute-start | bytes 294920 | tf_op jit(solution)/shard_map/ppermute | solution.py:12
  (65 other events, 300.2 us)
Sparse Core Ops, SparseCore 0:
  134.9 46.5 all-gather.6
  208.3 51.0 all-gather.4
  453.8 132.8 all-reduce.29
where the time goes:
time: 608 us; the launch traced here: 597 us
  other arithmetic  254 us (42%)
  waiting for transfers between devices  160 us (26%)
  local copies, waits for them, and re-layouts  95.1 us (16%)
  blocking collectives  55.6 us (9%)
  between operations  17.1 us (3%)
  starting transfers between devices  15.7 us (3%)
    psum x1, waiting for transfers between devices, shards(): lax.psum((jnp.stack(tap_terms, axis=1), skip_term, residue_term), ('dp',...  122 us
    add x32, other arithmetic, advance(): return (term + decay_block * passed[:, None, None] * carried, carried)  79.9 us
    psum x1, blocking collectives, shards(): lax.psum((jnp.stack(tap_terms, axis=1), skip_term, residue_term), ('dp',...  36.9 us
    dynamic_slice x32, local copies, waits for them, and re-layouts, sweep(): return lax.scan(advance, initial, (pass_sub.T, terms), reverse=reverse_flag)  32.9 us
    all_gather x1, waiting for transfers between devices, shards(): sums = lax.all_gather(block_sum[None], 'ctx', axis=0, tiled=True)  31.7 us
    dynamic_update_slice x16, local copies, waits for them, and re-layouts, sweep(): return lax.scan(advance, initial, (pass_sub.T, terms), reverse=reverse_flag)  26.8 us
    reduce_sum x2, other arithmetic, shards(): tap_terms.append(jnp.sum(window(tap_index) * short_grads, axis=(1, 2)))  19.4 us
    unnamed x1, blocking collectives  18.6 us
  transfers between devices with their start and end apart: 9, of which 5 were waited for; matrix products, arithmetic and copies ran while one was open for 14% of the time, Pallas kernels for 0%

commit v1 on v0

v1 whole, which is shorter than its diff:
```python
import functools
import math

import jax
import jax.numpy as jnp
from jax import lax
from jax.experimental import pallas as pl
from jax.experimental.pallas import tpu as pltpu
from jax.sharding import PartitionSpec as P

F32 = jnp.float32
BF16 = jnp.bfloat16
SUB = 8
LANES = 128
MESH = pl.DeviceIdType.MESH


def decay_powers(lam):
    powers = [jnp.ones_like(lam)]
    for _ in range(SUB - 1):
        powers.append(powers[-1] * lam)
    return powers


def cols_of(step):
    return pl.ds(pl.multiple_of(step * LANES, LANES), LANES)


def fill_extended(ext_ref, branch, rim_ref, source, cols):
    ext_ref[branch, 0:SUB, :] = rim_ref[branch, :, cols]
    ext_ref[branch, SUB:, :] = source


def local_kernel(
    taps,
    q_ref,
    k_ref,
    v_ref,
    og_ref,
    rim_ref,
    offs_ref,
    valid_ref,
    last_ref,
    pass_ref,
    short_ref,
    lamlog_ref,
    qs_ref,
    ks_ref,
    vs_ref,
    sig_ref,
    gam_ref,
    bsum_ref,
    badj_ref,
    ext_ref,
    xm_ref,
    zm_ref,
):
    tok, width = q_ref.shape

    def subtile(step, carry):
        cols = cols_of(step)
        offs = offs_ref[...]
        outs = []
        for branch, (ref, out) in enumerate(((q_ref, qs_ref), (k_ref, ks_ref), (v_ref, vs_ref))):
            source = ref[:, cols].astype(F32)
            fill_extended(ext_ref, branch, rim_ref, source, cols)
            total = short_ref[branch, 0:1, cols] * source
            for tap in range(1, taps):
                window = ext_ref[branch, SUB - tap : SUB - tap + tok, :]
                total = total + short_ref[branch, tap : tap + 1, cols] * jnp.where(
                    offs >= float(tap), window, 0.0
                )
            out[:, cols] = total
            outs.append(total)
        xm_ref[...] = outs[1] * outs[2] * last_ref[...]
        zm_ref[...] = og_ref[:, cols].astype(F32) * outs[0] * valid_ref[...]
        lam = jnp.exp(lamlog_ref[:, cols])
        powers = decay_powers(lam)
        span = powers[SUB - 1] * lam

        def sub_block(block, state):
            total, adjoint, weight = state
            base = block * SUB
            sigma = xm_ref[pl.ds(base + SUB - 1, 1), :] * powers[0]
            gamma = zm_ref[pl.ds(base, 1), :] * powers[0]
            for pos in range(1, SUB):
                sigma = sigma + powers[pos] * xm_ref[pl.ds(base + SUB - 1 - pos, 1), :]
                gamma = gamma + powers[pos] * zm_ref[pl.ds(base + pos, 1), :]
            sig_ref[block, :, cols] = sigma
            gam_ref[block, :, cols] = gamma
            factor = span * pass_ref[pl.ds(block, 1), :]
            return (sigma + factor * total, adjoint + weight * gamma, weight * factor)

        zero = jnp.zeros_like(lam)
        total, adjoint, _ = lax.fori_loop(
            0, tok // SUB, sub_block, (zero, zero, jnp.ones_like(lam)), unroll=4
        )
        bsum_ref[:, cols] = total
        badj_ref[:, cols] = adjoint
        return carry

    lax.fori_loop(0, width // LANES, subtile, 0)


def main_kernel(
    taps,
    q_ref,
    k_ref,
    v_ref,
    og_ref,
    rim_ref,
    qs_ref,
    ks_ref,
    vs_ref,
    sig_ref,
    gam_ref,
    enter_ref,
    adj_ref,
    offx_ref,
    offin_ref,
    valid_ref,
    last_ref,
    pass_ref,
    short_ref,
    lamlog_ref,
    coef_ref,
    norm_ref,
    skip_ref,
    mo_ref,
    qg_ref,
    kg_ref,
    vg_ref,
    head_ref,
    tail_ref,
    acc_ref,
    src_ref,
    g_ref,
    mo_scr,
    enters_scr,
    exits_scr,
    fwd_scr,
    bwd_scr,
    filt_scr,
):
    tok, width = q_ref.shape
    blocks = tok // SUB
    modes = lamlog_ref.shape[0]
    rows = lax.broadcasted_iota(jnp.int32, (SUB, LANES), 0).astype(F32)

    def subtile(step, carry):
        cols = cols_of(step)
        lamlog = lamlog_ref[:, cols]
        coef = coef_ref[:, cols]
        lam = jnp.exp(lamlog)
        powers = decay_powers(lam)
        span = powers[SUB - 1] * lam
        for lag in range(SUB):
            filt_scr[lag : lag + 1, :] = jnp.sum(coef * powers[lag], axis=0, keepdims=True)
        for mode in range(modes):
            log_row = lamlog[mode : mode + 1, :]
            coef_row = coef[mode : mode + 1, :]
            fwd_scr[mode] = coef_row * jnp.exp(log_row * (rows + 1.0))
            bwd_scr[mode] = coef_row * jnp.exp(log_row * (float(SUB) - rows))

        def sweep(index, state):
            forward, backward = state
            back = blocks - 1 - index
            enters_scr[index] = forward
            exits_scr[back] = backward
            forward = sig_ref[index, :, cols] + span * pass_ref[pl.ds(index, 1), :] * forward
            backward = gam_ref[back, :, cols] + span * pass_ref[pl.ds(back, 1), :] * backward
            return forward, backward

        lax.fori_loop(0, blocks, sweep, (enter_ref[:, cols], adj_ref[:, cols]), unroll=4)

        for branch, ref in enumerate((q_ref, k_ref, v_ref)):
            fill_extended(src_ref, branch, rim_ref, ref[:, cols].astype(F32), cols)
            g_ref[branch, 0:SUB, :] = jnp.zeros((SUB, LANES), F32)
            g_ref[branch, SUB + tok :, :] = jnp.zeros((SUB, LANES), F32)
        mo_scr[...] = og_ref[:, cols].astype(F32)
        skip = skip_ref[:, cols]

        def sub_block(block, state):
            lag_sums, res = state
            at = pl.ds(pl.multiple_of(block * SUB, SUB), SUB)
            query = qs_ref[at, cols]
            key = ks_ref[at, cols]
            value = vs_ref[at, cols]
            grad = mo_scr[at, :]
            mixed = key * value
            z_grad = grad * query
            offin = offin_ref[at, :]
            cross = jnp.zeros((SUB, LANES), F32)
            cross_back = jnp.zeros((SUB, LANES), F32)
            for mode in range(modes):
                cross = cross + fwd_scr[mode] * enters_scr[block, mode : mode + 1, :]
                cross_back = cross_back + bwd_scr[mode] * exits_scr[block, mode : mode + 1, :]
            first = filt_scr[0:1, :]
            forward = valid_ref[at, :] * cross + (first + skip) * mixed
            backward = last_ref[at, :] * cross_back + (first + skip) * z_grad
            new_sums = [lag_sums[0] + z_grad * mixed]
            for lag in range(1, SUB):
                inside = offin >= float(lag)
                tap = filt_scr[lag : lag + 1, :]
                shifted = jnp.where(inside, pltpu.roll(mixed, lag, 0), 0.0)
                forward = forward + tap * shifted
                new_sums.append(lag_sums[lag] + z_grad * shifted)
                backward = backward + tap * pltpu.roll(
                    jnp.where(inside, z_grad, 0.0), SUB - lag, 0
                )
            res = res + gam_ref[block, :, cols] * enters_scr[block]
            mo_scr[at, :] = query * forward
            put = pl.ds(pl.multiple_of(block * SUB + SUB, SUB), SUB)
            g_ref[0, put, :] = grad * forward
            g_ref[1, put, :] = backward * value
            g_ref[2, put, :] = backward * key
            return tuple(new_sums), res

        lag_sums, res = lax.fori_loop(
            0,
            blocks,
            sub_block,
            (
                tuple(jnp.zeros((SUB, LANES), F32) for _ in range(SUB)),
                jnp.zeros((modes, LANES), F32),
            ),
            unroll=2,
        )
        mo_ref[:, cols] = mo_scr[...].astype(BF16)
        res = res * lam
        sums = [jnp.sum(lag_sum, axis=0, keepdims=True) for lag_sum in lag_sums]
        for lag in range(SUB):
            res = res + powers[lag] * sums[lag]
        skip_row = 3 * taps
        res_row = acc_ref.shape[0] - modes
        acc_ref[skip_row:res_row, cols] = jnp.concatenate(
            [sums[0], jnp.zeros((res_row - skip_row - 1, LANES), F32)], axis=0
        )
        acc_ref[res_row:, cols] = norm_ref[:, cols] * res

        span_rows = tok + SUB
        for branch, out in enumerate((qg_ref, kg_ref, vg_ref)):
            source = src_ref[branch]
            spread = jnp.zeros((span_rows, LANES), F32)
            for tap in range(taps):
                moved = g_ref[branch, tap : tap + span_rows, :]
                if tap > 0:
                    moved = jnp.where(offx_ref[tap : tap + span_rows, :] >= float(tap), moved, 0.0)
                spread = spread + short_ref[branch, tap : tap + 1, cols] * moved
                row = branch * taps + tap
                acc_ref[row : row + 1, cols] = jnp.sum(source * moved, axis=0, keepdims=True)
            head_ref[branch, :, cols] = spread[0:SUB, :]
            out[:, cols] = spread[SUB:, :].astype(BF16)
            tail_ref[branch, :, cols] = spread[span_rows - 2 * SUB :, :]
        return carry

    lax.fori_loop(0, width // LANES, subtile, 0)


def hop_list(count):
    hops = [1]
    reach = 1
    while reach < count - 1:
        hops.append(reach)
        reach *= 2
    return hops


def state_kernel(
    tok,
    count,
    chunks,
    bsum_ref,
    badj_ref,
    lamlog_ref,
    mask_ref,
    enter_ref,
    adj_ref,
    fsend,
    frecv,
    bsend,
    brecv,
    fsem_s,
    fsem_r,
    bsem_s,
    bsem_r,
):
    hops = hop_list(count)
    me = lax.axis_index("ctx")
    barrier = pltpu.get_barrier_semaphore()
    partners = 0
    for hop in sorted(set(hops)):
        for sign in (1, -1):
            other = me + sign * hop
            there = jnp.logical_and(other >= 0, other < count)

            @pl.when(there)
            def _():
                pl.semaphore_signal(
                    barrier, inc=1, device_id={"ctx": other}, device_id_type=MESH
                )

            partners = partners + there.astype(jnp.int32)
    pl.semaphore_wait(barrier, partners)
    width = bsum_ref.shape[1] // chunks

    def copies(step, chunk):
        hop = hops[step]
        forward = pltpu.make_async_remote_copy(
            src_ref=fsend.at[step, chunk],
            dst_ref=frecv.at[step, chunk],
            send_sem=fsem_s.at[step, chunk],
            recv_sem=fsem_r.at[step, chunk],
            device_id={"ctx": me + hop},
            device_id_type=MESH,
        )
        backward = pltpu.make_async_remote_copy(
            src_ref=bsend.at[step, chunk],
            dst_ref=brecv.at[step, chunk],
            send_sem=bsem_s.at[step, chunk],
            recv_sem=bsem_r.at[step, chunk],
            device_id={"ctx": me - hop},
            device_id_type=MESH,
        )
        return forward, backward, me + hop < count, me - hop >= 0

    def start(step, chunk):
        forward, backward, upper, lower = copies(step, chunk)

        @pl.when(upper)
        def _():
            forward.start()

        @pl.when(lower)
        def _():
            backward.start()

    def mask_row(row):
        return jnp.concatenate([mask_ref[row : row + 1, :]] * (width // LANES), axis=1)

    steps = len(hops)
    for chunk in range(chunks):
        cols = slice(chunk * width, (chunk + 1) * width)
        fsend[0, chunk] = bsum_ref[:, cols]
        bsend[0, chunk] = badj_ref[:, cols] * mask_row(steps)
        start(0, chunk)
    for step in range(steps):
        for chunk in range(chunks):
            cols = slice(chunk * width, (chunk + 1) * width)
            forward, backward, upper, lower = copies(step, chunk)
            fmask = mask_row(step)
            if step > 0:
                decay = jnp.exp(float(tok * hops[step]) * lamlog_ref[:, cols])

            @pl.when(lower)
            def _():
                forward.wait_recv()
                if step == 0:
                    enter_ref[:, cols] = fmask * frecv[step, chunk]
                else:
                    enter_ref[:, cols] = (
                        enter_ref[:, cols] + decay * fmask * frecv[step, chunk]
                    )

            if step == 0:

                @pl.when(jnp.logical_not(lower))
                def _():
                    enter_ref[:, cols] = jnp.zeros((bsum_ref.shape[0], width), F32)

                @pl.when(jnp.logical_not(upper))
                def _():
                    adj_ref[:, cols] = jnp.zeros((bsum_ref.shape[0], width), F32)

            @pl.when(upper)
            def _():
                backward.wait_recv()
                if step == 0:
                    adj_ref[:, cols] = brecv[step, chunk]
                else:
                    adj_ref[:, cols] = adj_ref[:, cols] + decay * brecv[step, chunk]

            if step + 1 < steps:
                fsend[step + 1, chunk] = enter_ref[:, cols]
                bsend[step + 1, chunk] = adj_ref[:, cols] * mask_row(steps + step + 1)
                start(step + 1, chunk)
    for step in range(steps):
        for chunk in range(chunks):
            forward, backward, upper, lower = copies(step, chunk)

            @pl.when(upper)
            def _():
                forward.wait_send()

            @pl.when(lower)
            def _():
                backward.wait_send()


def reduce_kernel(
    dp_count,
    ctx_count,
    scale,
    acc_ref,
    out_ref,
    dp_recv,
    part,
    ctx_recv,
    full,
    s1,
    r1,
    s2,
    r2,
    s3,
    r3,
    s4,
    r4,
):
    dp = lax.axis_index("dp")
    ctx = lax.axis_index("ctx")
    channels = acc_ref.shape[1]
    wide = channels // dp_count
    narrow = wide // ctx_count
    barrier = pltpu.get_barrier_semaphore()
    for step in range(1, dp_count):
        pl.semaphore_signal(
            barrier, 1, device_id={"dp": (dp + step) % dp_count}, device_id_type=MESH
        )
    for step in range(1, ctx_count):
        pl.semaphore_signal(
            barrier, 1, device_id={"ctx": (ctx + step) % ctx_count}, device_id_type=MESH
        )
    pl.semaphore_wait(barrier, dp_count + ctx_count - 2)

    def wide_cols(index):
        return pl.ds(pl.multiple_of(index * wide, wide), wide)

    def narrow_cols(index):
        return pl.ds(pl.multiple_of(index * narrow, narrow), narrow)

    sent = []
    for step in range(1, dp_count):
        peer = (dp + step) % dp_count
        copy = pltpu.make_async_remote_copy(
            src_ref=acc_ref.at[:, wide_cols(peer)],
            dst_ref=dp_recv.at[step - 1],
            send_sem=s1.at[step - 1],
            recv_sem=r1.at[step - 1],
            device_id={"dp": peer},
            device_id_type=MESH,
        )
        copy.start()
        sent.append(copy)
    total = acc_ref[:, wide_cols(dp)]
    for step, copy in enumerate(sent):
        copy.wait_recv()
        total = total + dp_recv[step]
    part[...] = total
    ring = []
    for step in range(1, ctx_count):
        peer = (ctx + step) % ctx_count
        copy = pltpu.make_async_remote_copy(
            src_ref=part.at[:, narrow_cols(peer)],
            dst_ref=ctx_recv.at[step - 1],
            send_sem=s2.at[step - 1],
            recv_sem=r2.at[step - 1],
            device_id={"ctx": peer},
            device_id_type=MESH,
        )
        copy.start()
        ring.append(copy)
    total = part[:, narrow_cols(ctx)]
    for step, copy in enumerate(ring):
        copy.wait_recv()
        total = total + ctx_recv[step]
    mine = pl.ds(pl.multiple_of(dp * wide + ctx * narrow, narrow), narrow)
    full[:, mine] = total * scale
    sent += ring
    ring = []
    for step in range(1, ctx_count):
        peer = (ctx + step) % ctx_count
        copy = pltpu.make_async_remote_copy(
            src_ref=full.at[:, mine],
            dst_ref=full.at[:, mine],
            send_sem=s3.at[step - 1],
            recv_sem=r3.at[step - 1],
            device_id={"ctx": peer},
            device_id_type=MESH,
        )
        copy.start()
        ring.append(copy)
    for copy in ring:
        copy.wait_recv()
    sent += ring
    ring = []
    for step in range(1, dp_count):
        peer = (dp + step) % dp_count
        copy = pltpu.make_async_remote_copy(
            src_ref=full.at[:, wide_cols(dp)],
            dst_ref=full.at[:, wide_cols(dp)],
            send_sem=s4.at[step - 1],
            recv_sem=r4.at[step - 1],
            device_id={"dp": peer},
            device_id_type=MESH,
        )
        copy.start()
        ring.append(copy)
    for copy in ring:
        copy.wait_recv()
    out_ref[...] = full[...]
    for copy in sent + ring:
        copy.wait_send()


def reduce_all(acc, scale):
    dp_count = lax.axis_size("dp")
    ctx_count = lax.axis_size("ctx")
    rows, channels = acc.shape
    if channels % (dp_count * ctx_count * LANES) != 0:
        return lax.psum(acc, ("dp", "ctx")) * scale
    wide = channels // dp_count
    narrow = wide // ctx_count
    dma = pltpu.SemaphoreType.DMA
    return pl.pallas_call(
        functools.partial(reduce_kernel, dp_count, ctx_count, scale),
        out_shape=jax.ShapeDtypeStruct(acc.shape, F32),
        in_specs=[pl.BlockSpec(memory_space=pltpu.VMEM)],
        out_specs=pl.BlockSpec(memory_space=pltpu.VMEM),
        scratch_shapes=[
            pltpu.VMEM((dp_count - 1, rows, wide), F32),
            pltpu.VMEM((rows, wide), F32),
            pltpu.VMEM((ctx_count - 1, rows, narrow), F32),
            pltpu.VMEM((rows, channels), F32),
            dma((dp_count - 1,)),
            dma((dp_count - 1,)),
            dma((ctx_count - 1,)),
            dma((ctx_count - 1,)),
            dma((ctx_count - 1,)),
            dma((ctx_count - 1,)),
            dma((dp_count - 1,)),
            dma((dp_count - 1,)),
        ],
        compiler_params=pltpu.CompilerParams(
            collective_id=1, has_side_effects=True, vmem_limit_bytes=16 << 20
        ),
        name="reduce_grads",
    )(acc)


def exchange_states(tok, bsum, badj, lam_log, masks):
    count = lax.axis_size("ctx")
    steps = len(hop_list(count))
    chunks = 2
    modes, channels = bsum.shape
    dma = pltpu.SemaphoreType.DMA
    slot = pltpu.VMEM((steps, chunks, modes, channels // chunks), F32)
    return pl.pallas_call(
        functools.partial(state_kernel, tok, count, chunks),
        out_shape=[jax.ShapeDtypeStruct(bsum.shape, F32)] * 2,
        in_specs=[pl.BlockSpec(memory_space=pltpu.VMEM)] * 4,
        out_specs=[pl.BlockSpec(memory_space=pltpu.VMEM)] * 2,
        scratch_shapes=[slot] * 4 + [dma((steps, chunks))] * 4,
        compiler_params=pltpu.CompilerParams(
            collective_id=0, has_side_effects=True, vmem_limit_bytes=24 << 20
        ),
        name="exchange_states",
    )(bsum, badj, lam_log, masks)


def from_behind(block, distance):
    devices = range(lax.axis_size("ctx"))
    route = [(i - distance, i) for i in devices if i - distance in devices]
    return lax.ppermute(block, "ctx", route)


def shards(
    query_proj,
    key_proj,
    value_proj,
    doc_offset,
    short_taps,
    rate_scale,
    residue,
    skip_gain,
    out_grad,
):
    row_count, tok, channels = query_proj.shape
    ctx_count = lax.axis_size("ctx")
    seq_len = tok * ctx_count
    total_tokens = row_count * lax.axis_size("dp") * seq_len
    taps = short_taps.shape[1]
    modes = rate_scale.shape[0]
    rim = taps - 1
    blocks = tok // SUB
    query, key, value, grad = query_proj[0], key_proj[0], value_proj[0], out_grad[0]
    edge = jnp.stack([query[tok - rim :], key[tok - rim :], value[tok - rim :]], axis=0)
    edge = from_behind(edge, 1)
    edge = jnp.pad(edge.astype(F32), ((0, 0), (SUB - rim, 0), (0, 0)))

    lam_log = -rate_scale / seq_len
    norm = jnp.sqrt(-jnp.expm1(2.0 * lam_log))
    coef = residue * norm

    offs = doc_offset[0]
    index = jnp.arange(tok, dtype=jnp.int32) % SUB
    ends = offs.reshape(blocks, SUB)[:, SUB - 1]

    def wide(values):
        return jnp.broadcast_to(values.astype(F32)[:, None], (values.shape[0], LANES))

    offs_wide = wide(offs)
    offs_ext = jnp.pad(offs_wide, ((SUB, SUB), (0, 0)))
    offs_in = wide(jnp.minimum(offs, index))
    valid = wide(offs > index)
    last = wide(index >= SUB - 1 - jnp.repeat(ends, SUB))
    passes = wide(ends >= SUB)
    hops = hop_list(ctx_count)
    receive = [offs[0] >= 1] + [offs[0] >= tok * hop + 1 for hop in hops[1:]]
    send = [offs[0] >= 1] + [offs[tok - 1] >= tok * hop for hop in hops[1:]]
    masks = wide(jnp.stack(receive + send))

    width = 512 if channels % 512 == 0 else LANES
    grid = (channels // width,)

    def tile(*lead):
        zeros = (0,) * len(lead)
        return pl.BlockSpec(lead + (width,), lambda i: zeros + (i,))

    def whole(array):
        zeros = (0,) * array.ndim
        return pl.BlockSpec(array.shape, lambda i: zeros)

    def out(*dims, dtype=F32):
        return jax.ShapeDtypeStruct(dims + (channels,), dtype)

    token_tile = tile(tok)
    mode_tile = tile(modes)
    params = pltpu.CompilerParams(
        dimension_semantics=("arbitrary",), vmem_limit_bytes=48 << 20
    )
    qs, ks, vs, sig, gam, bsum, badj = pl.pallas_call(
        functools.partial(local_kernel, taps),
        grid=grid,
        out_shape=[out(tok)] * 3 + [out(blocks, modes)] * 2 + [out(modes)] * 2,
        in_specs=[token_tile] * 4
        + [tile(3, SUB)]
        + [whole(a) for a in (offs_wide, valid, last, passes)]
        + [tile(3, taps), mode_tile],
        out_specs=[token_tile] * 3 + [tile(blocks, modes)] * 2 + [mode_tile] * 2,
        scratch_shapes=[
            pltpu.VMEM((3, SUB + tok, LANES), F32),
            pltpu.VMEM((tok, LANES), F32),
            pltpu.VMEM((tok, LANES), F32),
        ],
        compiler_params=params,
        name="local_states",
    )(query, key, value, grad, edge, offs_wide, valid, last, passes, short_taps, lam_log)

    enter, adj = exchange_states(tok, bsum, badj, lam_log, masks)

    acc_rows = -(-(3 * taps + 1) // SUB) * SUB + modes
    skip_row = skip_gain[None, :]
    mixed_out, qg, kg, vg, heads, tails, acc = pl.pallas_call(
        functools.partial(main_kernel, taps),
        grid=grid,
        out_shape=[out(tok, dtype=BF16)] * 4 + [out(3, SUB), out(3, 2 * SUB), out(acc_rows)],
        in_specs=[token_tile] * 4
        + [tile(3, SUB)]
        + [token_tile] * 3
        + [tile(blocks, modes)] * 2
        + [mode_tile] * 2
        + [whole(a) for a in (offs_ext, offs_in, valid, last, passes)]
        + [tile(3, taps)]
        + [mode_tile] * 3
        + [tile(1)],
        out_specs=[token_tile] * 4 + [tile(3, SUB), tile(3, 2 * SUB), tile(acc_rows)],
        scratch_shapes=[
            pltpu.VMEM((3, SUB + tok, LANES), F32),
            pltpu.VMEM((3, tok + 2 * SUB, LANES), F32),
            pltpu.VMEM((tok, LANES), F32),
            pltpu.VMEM((blocks, modes, LANES), F32),
            pltpu.VMEM((blocks, modes, LANES), F32),
            pltpu.VMEM((modes, SUB, LANES), F32),
            pltpu.VMEM((modes, SUB, LANES), F32),
            pltpu.VMEM((SUB, LANES), F32),
        ],
        compiler_params=params,
        name="main_grads",
    )(
        query,
        key,
        value,
        grad,
        edge,
        qs,
        ks,
        vs,
        sig,
        gam,
        enter,
        adj,
        offs_ext,
        offs_in,
        valid,
        last,
        passes,
        short_taps,
        lam_log,
        coef,
        norm,
        skip_row,
    )
    incoming = from_behind(heads, -1)
    fixed = (tails + jnp.pad(incoming, ((0, 0), (SUB, 0), (0, 0)))).astype(BF16)
    grads = [
        lax.dynamic_update_slice(g, fixed[branch], (tok - 2 * SUB, 0))[None]
        for branch, g in enumerate((qg, kg, vg))
    ]
    sums = reduce_all(acc, 1.0 / math.sqrt(total_tokens))
    return (
        mixed_out[None],
        grads[0],
        grads[1],
        grads[2],
        sums[: 3 * taps].reshape(3, taps, channels),
        sums[3 * taps],
        sums[acc_rows - modes :],
    )


def solution(mesh):
    tokens = P("dp", "ctx", None)
    in_specs = (tokens, tokens, tokens, P("dp", "ctx"), P(), P(), P(), P(), tokens)
    out_specs = (tokens, tokens, tokens, tokens, P(), P(), P())
    return jax.shard_map(shards, mesh=mesh, in_specs=in_specs, out_specs=out_specs, check_vma=False)
```

time: 608 us -> 152 us (0.25); the launches traced: 597 us -> 151 us
  other arithmetic: 254 us -> 5.31 us
  waiting for transfers between devices: 160 us -> 0.01 us
  Pallas kernels: 0 us -> 123 us
  local copies, waits for them, and re-layouts: 95.1 us -> 10 us
  blocking collectives: 55.6 us -> 0 us
  between operations: 17.1 us -> 5.33 us
  starting transfers between devices: 15.7 us -> 6.84 us
    pallas_call x0 -> x4, Pallas kernels: none -> 123 us  [the longest x1 42.8 us: exchange_states(): pl.pallas_call(functools.partial(state_kernel, tok, count, chunks), out_s...]
    psum x1 -> x0, waiting for transfers between devices: 122 us -> none  [shards(): lax.psum((jnp.stack(tap_terms, axis=1), skip_term, residue_term), ('dp',...]
    add x36 -> x0, other arithmetic: 121 us -> none  [the longest x32 79.9 us: advance(): return (term + decay_block * passed[:, None, None] * carried, carried)]
    reduce_sum x11 -> x0, other arithmetic: 65.5 us -> none  [the longest x2 19.4 us: shards(): tap_terms.append(jnp.sum(window(tap_index) * short_grads, axis=(1, 2)))]
    psum x1 -> x0, blocking collectives: 36.9 us -> none  [shards(): lax.psum((jnp.stack(tap_terms, axis=1), skip_term, residue_term), ('dp',...]
    dynamic_slice x32 -> x0, local copies, waits for them, and re-layouts: 32.9 us -> none  [sweep(): return lax.scan(advance, initial, (pass_sub.T, terms), reverse=reverse_flag)]
    all_gather x2 -> x0, waiting for transfers between devices: 31.7 us -> none  [the longest x1 31.7 us: shards(): sums = lax.all_gather(block_sum[None], 'ctx', axis=0, tiled=True)]
    dynamic_update_slice x16 -> x1, local copies, waits for them, and re-layouts: 26.8 us -> 0.75 us  [shards(): lax.dynamic_update_slice(g, fixed[branch], (tok - 2 * SUB, 0))[None]]
  transfers between devices with their start and end apart: 9 -> 2, of which waited for: 5 -> 0; matrix products, arithmetic and copies ran while one was open for 14% -> 5% of each run, Pallas kernels for 0% -> 19%
where the time goes in v1:
time: 152 us; the launch traced here: 151 us
  Pallas kernels  123 us (81%)
  local copies, waits for them, and re-layouts  10 us (7%)
  starting transfers between devices  6.84 us (4%)
  between operations  5.33 us (4%)
  other arithmetic  5.31 us (3%)
    pallas_call x1, Pallas kernels, exchange_states(): pl.pallas_call(functools.partial(state_kernel, tok, count, chunks), out_s...  42.8 us
    pallas_call x1, Pallas kernels, shards(): pl.pallas_call(functools.partial(main_kernel, taps), grid=grid, out_shape...  36.9 us
    pallas_call x1, Pallas kernels, reduce_all(): pl.pallas_call(functools.partial(reduce_kernel, dp_count, ctx_count, scal...  28.3 us
    pallas_call x1, Pallas kernels, shards(): pl.pallas_call(functools.partial(local_kernel, taps), grid=grid, out_shap...  15.1 us
    ppermute x2, starting transfers between devices, from_behind(): return lax.ppermute(block, 'ctx', route)  6.84 us
  transfers between devices with their start and end apart: 2, of which 0 were waited for; matrix products, arithmetic and copies ran while one was open for 5% of the time, Pallas kernels for 19%

profile of v1, /device:TPU:0, one launch (start us, length us, event | category | flops | bytes accessed | tf_op | source)
XLA Modules:
  0.0 150.7 jit_solution(2654237152168087002)
XLA Ops:
  0.6 0.0 copy-start
  0.6 0.0 copy-start.1
  0.7 0.0 copy-start.6
  0.7 0.0 copy-start.4
  0.7 1.0 slice.47
  1.7 0.9 slice.48
  2.5 0.9 slice.49
  3.5 5.5 %collective-permute-start = (bf16[3,6,4096]{2,1,0:T(8,128)(2,1)S(1)}, bf16[3,6,4096]{2,1,0:T(8,128)(2,1)}, u32[]{:S(2)}, u32[]{:S(2)}) collective-permute-start(bf16[3,6,4096]{2,1,0:T(8,128)(2,1)S(1)} %pad_maximum_fusion), channel_id=1, source_target_pairs={{0,1},{1,2},{2,3},{3,4},{4,5},{5,6},{6,7},{8,9},{9,10},{10,11},{11... | collective-permute-start | bytes 442376 | tf_op jit(solution)/shard_map/ppermute | solution.py:573
  9.0 0.7 fusion
  9.7 0.5 broadcast.74
  10.2 1.3 fusion.3
  11.5 0.1 reshape_squeeze.3
  11.6 0.2 subtract_reduce_fusion
  11.8 0.1 broadcast_in_dim.61
  11.8 0.1 sub.17
  12.0 0.7 compare_convert_fusion
  12.6 1.2 negate_sqrt_fusion
  13.8 0.0 copy-done.6
  13.8 0.6 fusion.2
  19.0 0.1 stack.39
  19.1 0.1 broadcast_in_dim.29.offs_ref
  19.2 0.2 convert_reduce_fusion
  19.3 0.0 collective-permute-done
  19.3 1.0 pad_convert_fusion.rim_ref
  20.3 0.1 broadcast_in_dim.65.pass_ref
  20.4 0.1 broadcast_in_dim.62.last_ref
  20.5 0.1 broadcast_in_dim.60.valid_ref
  20.6 0.0 copy-done
  20.6 0.0 copy-done.1
  20.6 0.0 copy-done.4
  20.6 0.0 copy-start.2
  20.6 1.2 copy-done.2
  21.8 0.0 copy-start.3
  21.8 1.2 copy-done.3
  23.1 15.1 %local_states.1 = (f32[128,4096]{1,0:T(8,128)}, f32[128,4096]{1,0:T(8,128)}, f32[128,4096]{1,0:T(8,128)}, f32[16,16,4096]{2,1,0:T(8,128)}, f32[16,16,4096]{2,1,0...) custom-call(bf16[128,4096]{1,0:T(8,128)(2,1)S(1)} %bitcast.23, bf16[128,4096]{1,0:T(8,128)(2,1)S(1)} %bitcast.26, ...), custom_call_target="tpu_custom_call" | custom-call | tf_op jit(solution)/shard_map/local_states/pallas_call | solution.py:641
  38.2 0.1 broadcast_in_dim.66.mask_ref
  38.3 42.8 %exchange_states.1 = (f32[16,4096]{1,0:T(8,128)S(1)}, f32[16,4096]{1,0:T(8,128)S(1)}) custom-call(f32[16,4096]{1,0:T(8,128)S(1)} %get-tuple-element.28.bsum_ref, f32[16,4096]{1,0:T(8,128)S(1)} %get-tuple-element.29.badj_ref, f32[16,4096]{1,0:T(8,128)S(1)} %get-tuple-element.44.lamlog_ref, f32[8,128]{1,0:T(8,128)S(1)} %broadcast_in_dim.66.mask_ref), custom_call_target="tpu_custom_call" | custom-call | tf_op jit(solution)/shard_map/exchange_states/pallas_call | solution.py:557
  81.1 0.1 broadcast_in_dim.67.offin_ref
  81.1 0.0 copy-done.5
  81.1 36.9 %main_grads.1 = (bf16[128,4096]{1,0:T(8,128)(2,1)}, bf16[128,4096]{1,0:T(8,128)(2,1)}, bf16[128,4096]{1,0:T(8,128)(2,1)}, bf16[128,4096]{1,0:T(8,128)(2,1)}, f32...) custom-call(bf16[128,4096]{1,0:T(8,128)(2,1)S(1)} %bitcast.24, bf16[128,4096]{1,0:T(8,128)(2,1)} %bitcast.25, ...), custom_call_target="tpu_custom_call" | custom-call | tf_op jit(solution)/shard_map/main_grads/pallas_call | solution.py:663
  118.1 1.3 collective-permute-start.1
  119.4 28.3 %reduce_grads.1 = f32[40,4096]{1,0:T(8,128)S(1)} custom-call(f32[40,4096]{1,0:T(8,128)S(1)} %get-tuple-element.38.acc_ref), custom_call_target="tpu_custom_call" | custom-call | tf_op jit(solution)/shard_map/reduce_grads/pallas_call | solution.py:524
  147.7 0.6 slice.57
  148.3 0.7 slice.58
  149.0 0.8 reshape.164
  149.8 0.0 collective-permute-done.1
  149.8 0.1 add_convert_fusion
  149.9 0.8 slice_dynamic-update-slice_fusion
  (5 shorter events, 0.1 us)
Async XLA Ops:
  0.6 19.9 %copy-start = (bf16[1,128,4096]{2,1,0:T(8,128)(2,1)S(1)}, bf16[1,128,4096]{2,1,0:T(8,128)(2,1)}, u32[]{:S(2)}) copy-start(bf16[1,128,4096]{2,1,0:T(8,128)(2,1)} %param.9) | copy-start | bytes 3145732
  0.6 19.9 %copy-start.1 = (bf16[1,128,4096]{2,1,0:T(8,128)(2,1)S(1)}, bf16[1,128,4096]{2,1,0:T(8,128)(2,1)}, u32[]{:S(2)}) copy-start(bf16[1,128,4096]{2,1,0:T(8,128)(2,1)} %param.10) | copy-start | bytes 3145732
  0.7 13.2 %copy-start.6 = (s32[1,128]{1,0:T(1,128)S(1)}, s32[1,128]{1,0:T(1,128)}, u32[]{:S(2)}) copy-start(s32[1,128]{1,0:T(1,128)} %param.12) | copy-start | bytes 1540
  0.7 19.9 %copy-start.4 = (f32[3,7,4096]{2,1,0:T(8,128)S(1)}, f32[3,7,4096]{2,1,0:T(8,128)}, u32[]{:S(2)}) copy-start(f32[3,7,4096]{2,1,0:T(8,128)} %short_ref.3) | copy-start | bytes 1032196
  3.5 15.9 %collective-permute-start = (bf16[3,6,4096]{2,1,0:T(8,128)(2,1)S(1)}, bf16[3,6,4096]{2,1,0:T(8,128)(2,1)}, u32[]{:S(2)}, u32[]{:S(2)}) collective-permute-start(bf16[3,6,4096]{2,1,0:T(8,128)(2,1)S(1)} %pad_maximum_fusion), channel_id=1, source_target_pairs={{0,1},{1,2},{2,3},{3,4},{4,5},{5,6},{6,7},{8,9},{9,10},{10,11},{11... | collective-permute-start | bytes 442376 | tf_op jit(solution)/shard_map/ppermute | solution.py:573
  20.6 1.2 copy-start.2
  21.8 1.2 copy-start.3
  23.0 58.1 %copy-start.5 = (f32[4096]{0:T(1024)S(1)}, f32[4096]{0:T(1024)}, u32[]{:S(2)}) copy-start(f32[4096]{0:T(1024)} %param.16) | copy-start | bytes 49156
  118.1 31.8 %collective-permute-start.1 = (f32[3,8,4096]{2,1,0:T(8,128)}, f32[3,8,4096]{2,1,0:T(8,128)S(1)}, u32[]{:S(2)}, u32[]{:S(2)}) collective-permute-start(f32[3,8,4096]{2,1,0:T(8,128)} %get-tuple-element.35), channel_id=1, source_target_pairs={{1,0},{2,1},{3,2},{4,3},{5,4},{6,5},{7,6},{9,8},{10,9},{11,10},{12... | collective-permute-start | bytes 1179656 | tf_op jit(solution)/shard_map/ppermute | solution.py:573

commit v2 on v0

v2 whole, which is shorter than its diff:
```python
import functools
import math

import jax
import jax.numpy as jnp
from jax import lax
from jax.experimental import pallas as pl
from jax.experimental.pallas import tpu as pltpu
from jax.sharding import PartitionSpec as P

F32 = jnp.float32
BF16 = jnp.bfloat16
SUB = 8
LANES = 128
MESH = pl.DeviceIdType.MESH


def decay_powers(lam):
    powers = [jnp.ones_like(lam)]
    for _ in range(SUB - 1):
        powers.append(powers[-1] * lam)
    return powers


def fused_kernel(
    cfg,
    q_ref,
    k_ref,
    v_ref,
    og_ref,
    offx_ref,
    offin_ref,
    valid_ref,
    last_ref,
    pass_ref,
    dev_ref,
    short_ref,
    lamlog_ref,
    coef_ref,
    norm_ref,
    skip_ref,
    mo_ref,
    qg_ref,
    kg_ref,
    vg_ref,
    taps_out,
    skip_out,
    res_out,
    qs_scr,
    ks_scr,
    vs_scr,
    sig_scr,
    gam_scr,
    rim_recv,
    ends,
    pair_recv,
    chain_out,
    chain_recv,
    flag_recv,
    head_send,
    head_recv,
    tail_scr,
    acc,
    dp_recv,
    part,
    ctx_recv,
    full,
    ext_ref,
    g_ref,
    xm_ref,
    zm_ref,
    enters_scr,
    exits_scr,
    fwd_scr,
    bwd_scr,
    filt_scr,
    flag_s,
    flag_r,
    rim_s,
    rim_r,
    pair_s,
    pair_r,
    ea_s,
    ea_r,
    eb_s,
    eb_r,
    head_s,
    head_r,
    s1,
    r1,
    s2,
    r2,
    s3,
    r3,
):
    taps, width, dp_count, count, fused, scale = cfg
    tok, channels = q_ref.shape
    modes = lamlog_ref.shape[0]
    blocks = tok // SUB
    chunks = channels // width
    tiles = width // LANES
    pairs = count // 2
    first_main = max(chunks, 2 + 2 * (pairs - 1))
    me = lax.axis_index("ctx")
    dp = lax.axis_index("dp")
    odd = me % 2
    pair = me // 2
    place = odd * pair + (1 - odd) * (pairs - 1 - pair)
    other_place = pairs - 1 - place
    lead = 2 * odd - 1
    partner = me - lead
    sources = (q_ref, k_ref, v_ref)
    rows = lax.broadcasted_iota(jnp.int32, (SUB, LANES), 0).astype(F32)

    barrier = pltpu.get_barrier_semaphore()
    if fused:
        others = dp_count * count - 1
        lin = dp * count + me

        def peer_of(step):
            peer = (lin + step) % (dp_count * count)
            return {"dp": peer // count, "ctx": peer % count}

        def greet(step, carry):
            pl.semaphore_signal(barrier, 1, device_id=peer_of(step), device_id_type=MESH)
            return carry

        lax.fori_loop(1, others + 1, greet, 0)
        pl.semaphore_wait(barrier, others)
    else:
        friends = 0
        for hop in (1, -1, 2, -2):
            friend = me + hop
            there = jnp.logical_and(friend >= 0, friend < count)

            @pl.when(there)
            def _():
                pl.semaphore_signal(
                    barrier, 1, device_id={"ctx": friend}, device_id_type=MESH
                )

            friends = friends + there.astype(jnp.int32)
        pl.semaphore_wait(barrier, friends)

    def remote(source, target, send, recv, device):
        return pltpu.make_async_remote_copy(
            src_ref=source,
            dst_ref=target,
            send_sem=send,
            recv_sem=recv,
            device_id=device,
            device_id_type=MESH,
        )

    def chunk_cols(chunk):
        return pl.ds(pl.multiple_of(chunk * width, width), width)

    def tile_cols(chunk, step):
        return pl.ds(pl.multiple_of(chunk * width + step * LANES, LANES), LANES)

    def lane_cols(step):
        return pl.ds(pl.multiple_of(step * LANES, LANES), LANES)

    def rim_copy(chunk, branch):
        return remote(
            sources[branch].at[tok - 2 * SUB : tok, chunk_cols(chunk)],
            rim_recv.at[chunk, branch],
            rim_s.at[chunk, branch],
            rim_r.at[chunk, branch],
            {"ctx": me + 1},
        )

    def pair_copy(chunk):
        return remote(
            ends.at[1 - odd, chunk],
            pair_recv.at[chunk],
            pair_s.at[chunk],
            pair_r.at[chunk],
            {"ctx": partner},
        )

    def chain_copy(chunk):
        return remote(
            chain_out.at[chunk],
            chain_recv.at[odd, chunk],
            ea_s.at[chunk],
            ea_r.at[chunk],
            {"ctx": me + 2 * lead},
        )

    def cross_copy(chunk):
        return remote(
            chain_out.at[chunk],
            chain_recv.at[odd, chunk],
            eb_s.at[chunk],
            eb_r.at[chunk],
            {"ctx": me + lead},
        )

    def cross_arrival(chunk):
        return remote(
            chain_out.at[chunk],
            chain_recv.at[1 - odd, chunk],
            eb_s.at[chunk],
            eb_r.at[chunk],
            {"ctx": me - lead},
        )

    def head_copy(chunk):
        return remote(
            head_send.at[chunk],
            head_recv.at[chunk],
            head_s.at[chunk],
            head_r.at[chunk],
            {"ctx": me - 1},
        )

    flag_copy = remote(dev_ref, flag_recv, flag_s, flag_r, {"ctx": partner})
    flag_copy.start()

    @pl.when(me + 1 < count)
    def _():
        def send(chunk, carry):
            for branch in range(3):
                rim_copy(chunk, branch).start()
            return carry

        lax.fori_loop(0, chunks, send, 0)

    @pl.when(me == 0)
    def _():
        rim_recv[...] = jnp.zeros(rim_recv.shape, BF16)

    @pl.when(place == 0)
    def _():
        chain_recv[odd] = jnp.zeros(chain_recv.shape[1:], F32)

    @pl.when(other_place == 0)
    def _():
        chain_recv[1 - odd] = jnp.zeros(chain_recv.shape[1:], F32)

    def fill(branch, chunk, step, cols):
        edge = rim_recv[chunk, branch, :, lane_cols(step)].astype(F32)
        ext_ref[branch, 0:SUB, :] = edge[SUB:, :]
        source = sources[branch][:, cols].astype(F32)
        ext_ref[branch, SUB:, :] = source
        return source

    def local_tile(chunk, step):
        cols = tile_cols(chunk, step)
        offs = offx_ref[SUB : SUB + tok, :]
        outs = []
        for branch, out in enumerate((qs_scr, ks_scr, vs_scr)):
            source = fill(branch, chunk, step, cols)
            total = short_ref[branch, 0:1, cols] * source
            for tap in range(1, taps):
                window = ext_ref[branch, SUB - tap : SUB - tap + tok, :]
                total = total + short_ref[branch, tap : tap + 1, cols] * jnp.where(
                    offs >= float(tap), window, 0.0
                )
            out[:, cols] = total
            outs.append(total)
        xm_ref[...] = outs[1] * outs[2] * last_ref[...]
        zm_ref[...] = og_ref[:, cols].astype(F32) * outs[0] * valid_ref[...]
        lam = jnp.exp(lamlog_ref[:, cols])
        powers = decay_powers(lam)
        span = powers[SUB - 1] * lam

        def sub_block(block, state):
            total, adjoint, weight = state
            base = block * SUB
            sigma = xm_ref[pl.ds(base + SUB - 1, 1), :] * powers[0]
            gamma = zm_ref[pl.ds(base, 1), :] * powers[0]
            for pos in range(1, SUB):
                sigma = sigma + powers[pos] * xm_ref[pl.ds(base + SUB - 1 - pos, 1), :]
                gamma = gamma + powers[pos] * zm_ref[pl.ds(base + pos, 1), :]
            sig_scr[block, :, cols] = sigma
            gam_scr[block, :, cols] = gamma
            factor = span * pass_ref[pl.ds(block, 1), :]
            return (sigma + factor * total, adjoint + weight * gamma, weight * factor)

        zero = jnp.zeros_like(lam)
        total, adjoint, _ = lax.fori_loop(
            0, blocks, sub_block, (zero, zero, jnp.ones_like(lam)), unroll=4
        )
        ends[1, chunk, :, lane_cols(step)] = total
        ends[0, chunk, :, lane_cols(step)] = adjoint

    def chain_tile(chunk, step):
        at = lane_cols(step)
        decay = jnp.exp(float(tok) * lamlog_ref[:, tile_cols(chunk, step)])
        state = (
            pair_recv[chunk, :, at]
            + decay * flag_recv[0:1, :] * chain_recv[odd, chunk, :, at]
        )
        chain_recv[odd, chunk, :, at] = state
        chain_out[chunk, :, at] = ends[odd, chunk, :, at] + decay * dev_ref[0:1, :] * state

    def main_tile(chunk, step):
        cols = tile_cols(chunk, step)
        at_lanes = lane_cols(step)
        lamlog = lamlog_ref[:, cols]
        coef = coef_ref[:, cols]
        lam = jnp.exp(lamlog)
        powers = decay_powers(lam)
        span = powers[SUB - 1] * lam
        for lag in range(SUB):
            filt_scr[lag : lag + 1, :] = jnp.sum(coef * powers[lag], axis=0, keepdims=True)
        for mode in range(modes):
            log_row = lamlog[mode : mode + 1, :]
            coef_row = coef[mode : mode + 1, :]
            fwd_scr[mode] = coef_row * jnp.exp(log_row * (rows + 1.0))
            bwd_scr[mode] = coef_row * jnp.exp(log_row * (float(SUB) - rows))

        def sweep(index, state):
            forward, backward = state
            back = blocks - 1 - index
            enters_scr[index] = forward
            exits_scr[back] = backward
            forward = sig_scr[index, :, cols] + span * pass_ref[pl.ds(index, 1), :] * forward
            backward = gam_scr[back, :, cols] + span * pass_ref[pl.ds(back, 1), :] * backward
            return forward, backward

        lax.fori_loop(
            0,
            blocks,
            sweep,
            (chain_recv[1, chunk, :, at_lanes], chain_recv[0, chunk, :, at_lanes]),
            unroll=4,
        )

        for branch in range(3):
            fill(branch, chunk, step, cols)
            g_ref[branch, 0:SUB, :] = jnp.zeros((SUB, LANES), F32)
            g_ref[branch, SUB + tok :, :] = jnp.zeros((SUB, LANES), F32)
        xm_ref[...] = og_ref[:, cols].astype(F32)
        skip = skip_ref[:, cols]

        def sub_block(block, state):
            lag_sums, res = state
            at = pl.ds(pl.multiple_of(block * SUB, SUB), SUB)
            query = qs_scr[at, cols]
            key = ks_scr[at, cols]
            value = vs_scr[at, cols]
            grad = xm_ref[at, :]
            mixed = key * value
            z_grad = grad * query
            offin = offin_ref[at, :]
            cross = jnp.zeros((SUB, LANES), F32)
            cross_back = jnp.zeros((SUB, LANES), F32)
            for mode in range(modes):
                cross = cross + fwd_scr[mode] * enters_scr[block, mode : mode + 1, :]
                cross_back = cross_back + bwd_scr[mode] * exits_scr[block, mode : mode + 1, :]
            first = filt_scr[0:1, :]
            forward = valid_ref[at, :] * cross + (first + skip) * mixed
            backward = last_ref[at, :] * cross_back + (first + skip) * z_grad
            new_sums = [lag_sums[0] + z_grad * mixed]
            for lag in range(1, SUB):
                inside = offin >= float(lag)
                tap = filt_scr[lag : lag + 1, :]
                shifted = jnp.where(inside, pltpu.roll(mixed, lag, 0), 0.0)
                forward = forward + tap * shifted
                new_sums.append(lag_sums[lag] + z_grad * shifted)
                backward = backward + tap * pltpu.roll(
                    jnp.where(inside, z_grad, 0.0), SUB - lag, 0
                )
            res = res + gam_scr[block, :, cols] * enters_scr[block]
            xm_ref[at, :] = query * forward
            put = pl.ds(pl.multiple_of(block * SUB + SUB, SUB), SUB)
            g_ref[0, put, :] = grad * forward
            g_ref[1, put, :] = backward * value
            g_ref[2, put, :] = backward * key
            return tuple(new_sums), res

        lag_sums, res = lax.fori_loop(
            0,
            blocks,
            sub_block,
            (
                tuple(jnp.zeros((SUB, LANES), F32) for _ in range(SUB)),
                jnp.zeros((modes, LANES), F32),
            ),
            unroll=2,
        )
        mo_ref[:, cols] = xm_ref[...].astype(BF16)
        res = res * lam
        sums = [jnp.sum(lag_sum, axis=0, keepdims=True) for lag_sum in lag_sums]
        for lag in range(SUB):
            res = res + powers[lag] * sums[lag]
        skip_row = 3 * taps
        res_row = acc.shape[1] - modes
        acc[chunk, skip_row:res_row, at_lanes] = jnp.concatenate(
            [sums[0], jnp.zeros((res_row - skip_row - 1, LANES), F32)], axis=0
        )
        acc[chunk, res_row:, at_lanes] = norm_ref[:, cols] * res

        span_rows = tok + SUB
        for branch, out in enumerate((qg_ref, kg_ref, vg_ref)):
            source = ext_ref[branch]
            spread = jnp.zeros((span_rows, LANES), F32)
            for tap in range(taps):
                moved = g_ref[branch, tap : tap + span_rows, :]
                if tap > 0:
                    moved = jnp.where(offx_ref[tap : tap + span_rows, :] >= float(tap), moved, 0.0)
                spread = spread + short_ref[branch, tap : tap + 1, cols] * moved
                row = branch * taps + tap
                acc[chunk, row : row + 1, at_lanes] = jnp.sum(
                    source * moved, axis=0, keepdims=True
                )
            head_send[chunk, branch, :, at_lanes] = spread[0:SUB, :]
            out[:, cols] = spread[SUB:, :].astype(BF16)
            tail_scr[chunk, branch, :, at_lanes] = spread[span_rows - 2 * SUB :, :]

    def each_tile(work, chunk):
        def one(step, carry):
            work(chunk, step)
            return carry

        lax.fori_loop(0, tiles, one, 0)

    def dp_copy(chunk, step):
        peer = (dp + step) % dp_count
        return remote(
            acc.at[chunk, :, lane_cols(peer)],
            dp_recv.at[chunk, step - 1],
            s1.at[chunk, step - 1],
            r1.at[chunk, step - 1],
            {"dp": peer},
        )

    def ctx_copy(chunk):
        slot = (me - chunk + count) % count - 1
        return remote(
            part.at[chunk], ctx_recv.at[slot], s2.at[chunk], r2.at[slot], {"ctx": chunk}
        )

    def ctx_arrival(slot):
        return remote(
            part.at[0], ctx_recv.at[slot], s2.at[0], r2.at[slot], {"ctx": partner}
        )

    mine = tile_cols(me, dp) if fused else None

    def spread_copy(step):
        return remote(
            full.at[:, mine], full.at[:, mine], s3.at[step - 1], r3.at[step - 1], peer_of(step)
        )

    flag_copy.wait()

    def slot_body(slot, carry):
        @pl.when(slot < chunks)
        def _():
            @pl.when(me > 0)
            def _():
                for branch in range(3):
                    rim_copy(slot, branch).wait_recv()

            each_tile(local_tile, slot)
            pair_copy(slot).start()

        link = slot - 2 - 2 * place

        @pl.when(jnp.logical_and(link >= 0, link < chunks))
        def _():
            pair_copy(link).wait_recv()

            @pl.when(place > 0)
            def _():
                chain_copy(link).wait_recv()

            each_tile(chain_tile, link)

            @pl.when(place < pairs - 1)
            def _():
                chain_copy(link).start()
                cross_copy(link).start()

        now = slot - first_main

        @pl.when(jnp.logical_and(now >= 0, now < chunks))
        def _():
            @pl.when(other_place > 0)
            def _():
                cross_arrival(now).wait_recv()

            each_tile(main_tile, now)

            @pl.when(me > 0)
            def _():
                head_copy(now).start()

            if fused:
                for step in range(1, dp_count):
                    dp_copy(now, step).start()

        done = now - 1

        @pl.when(jnp.logical_and(done >= 0, done < chunks))
        def _():
            if fused:
                total = acc[done, :, lane_cols(dp)]
                for step in range(1, dp_count):
                    dp_copy(done, step).wait_recv()
                    total = total + dp_recv[done, step - 1]
                part[done] = total

                @pl.when(done != me)
                def _():
                    ctx_copy(done).start()

            @pl.when(me + 1 < count)
            def _():
                head_copy(done).wait_recv()
                for branch, out in enumerate((qg_ref, kg_ref, vg_ref)):
                    tail = tail_scr[done, branch]
                    tail = jnp.concatenate(
                        [tail[0:SUB, :], tail[SUB:, :] + head_recv[done, branch]], axis=0
                    )
                    out[tok - 2 * SUB : tok, chunk_cols(done)] = tail.astype(BF16)

        if fused:

            @pl.when(now - 2 == me)
            def _():
                total = part[me]
                for index in range(count - 1):
                    ctx_arrival(index).wait_recv()
                    total = total + ctx_recv[index]
                full[:, mine] = total * scale

                def send(step, inner):
                    spread_copy(step).start()
                    return inner

                lax.fori_loop(1, others + 1, send, 0)

        return carry

    lax.fori_loop(0, first_main + chunks + 2, slot_body, 0)

    if fused:

        def arrive(step, carry):
            spread_copy(step).wait_recv()
            return carry

        lax.fori_loop(1, others + 1, arrive, 0)

    def emit(chunk, carry):
        cols = chunk_cols(chunk)
        sums = full[:, cols] if fused else acc[chunk]
        for branch in range(3):
            taps_out[branch, :, cols] = sums[branch * taps : (branch + 1) * taps, :]
        skip_out[:, cols] = sums[3 * taps : 3 * taps + 1, :]
        res_out[:, cols] = sums[sums.shape[0] - modes :, :]
        return carry

    lax.fori_loop(0, chunks, emit, 0)

    def drain(chunk, carry):
        pair_copy(chunk).wait_send()

        @pl.when(me + 1 < count)
        def _():
            for branch in range(3):
                rim_copy(chunk, branch).wait_send()

        @pl.when(place < pairs - 1)
        def _():
            chain_copy(chunk).wait_send()
            cross_copy(chunk).wait_send()

        @pl.when(me > 0)
        def _():
            head_copy(chunk).wait_send()

        if fused:
            for step in range(1, dp_count):
                dp_copy(chunk, step).wait_send()

            @pl.when(chunk != me)
            def _():
                ctx_copy(chunk).wait_send()

        return carry

    lax.fori_loop(0, chunks, drain, 0)
    if fused:

        def sent(step, carry):
            spread_copy(step).wait_send()
            return carry

        lax.fori_loop(1, others + 1, sent, 0)


def shards(
    query_proj,
    key_proj,
    value_proj,
    doc_offset,
    short_taps,
    rate_scale,
    residue,
    skip_gain,
    out_grad,
):
    row_count, tok, channels = query_proj.shape
    count = lax.axis_size("ctx")
    dp_count = lax.axis_size("dp")
    seq_len = tok * count
    scale = 1.0 / math.sqrt(row_count * dp_count * seq_len)
    taps = short_taps.shape[1]
    modes = rate_scale.shape[0]
    blocks = tok // SUB
    fused = channels == dp_count * count * LANES
    width = dp_count * LANES if fused else 4 * LANES
    chunks = channels // width

    lam_log = -rate_scale / seq_len
    norm = jnp.sqrt(-jnp.expm1(2.0 * lam_log))
    coef = residue * norm

    offs = doc_offset[0]
    index = jnp.arange(tok, dtype=jnp.int32) % SUB
    ends = offs.reshape(blocks, SUB)[:, SUB - 1]

    def wide(values):
        return jnp.broadcast_to(values.astype(F32)[:, None], (values.shape[0], LANES))

    offs_ext = jnp.pad(wide(offs), ((SUB, SUB), (0, 0)))
    offs_in = wide(jnp.minimum(offs, index))
    valid = wide(offs > index)
    last = wide(index >= SUB - 1 - jnp.repeat(ends, SUB))
    passes = wide(ends >= SUB)
    whole_doc = wide(jnp.broadcast_to(offs[tok - 1] >= tok, (SUB,)))

    acc_rows = -(-(3 * taps + 1) // SUB) * SUB + modes
    dma = pltpu.SemaphoreType.DMA
    vmem = pl.BlockSpec(memory_space=pltpu.VMEM)
    dp_steps, ctx_steps = max(dp_count - 1, 1), max(count - 1, 1)
    all_steps = dp_count * count - 1 if fused else 1

    def scr(*dims, dtype=F32):
        return pltpu.VMEM(dims, dtype)

    outs = pl.pallas_call(
        functools.partial(fused_kernel, (taps, width, dp_count, count, fused, scale)),
        out_shape=[jax.ShapeDtypeStruct((tok, channels), BF16)] * 4
        + [
            jax.ShapeDtypeStruct((3, taps, channels), F32),
            jax.ShapeDtypeStruct((1, channels), F32),
            jax.ShapeDtypeStruct((modes, channels), F32),
        ],
        in_specs=[vmem] * 15,
        out_specs=[vmem] * 7,
        scratch_shapes=[scr(tok, channels)] * 3
        + [scr(blocks, modes, channels)] * 2
        + [
            scr(chunks, 3, 2 * SUB, width, dtype=BF16),
            scr(2, chunks, modes, width),
            scr(chunks, modes, width),
            scr(chunks, modes, width),
            scr(2, chunks, modes, width),
            scr(SUB, LANES),
            scr(chunks, 3, SUB, width),
            scr(chunks, 3, SUB, width),
            scr(chunks, 3, 2 * SUB, width),
            scr(chunks, acc_rows, width),
            scr(chunks, dp_steps, acc_rows, LANES),
            scr(chunks, acc_rows, LANES),
            scr(ctx_steps, acc_rows, LANES),
            scr(acc_rows, channels),
            scr(3, SUB + tok, LANES),
            scr(3, tok + 2 * SUB, LANES),
            scr(tok, LANES),
            scr(tok, LANES),
            scr(blocks, modes, LANES),
            scr(blocks, modes, LANES),
            scr(modes, SUB, LANES),
            scr(modes, SUB, LANES),
            scr(SUB, LANES),
            dma,
            dma,
        ]
        + [dma((chunks, 3))] * 2
        + [dma((chunks,))] * 8
        + [dma((chunks, dp_steps))] * 2
        + [dma((chunks,)), dma((ctx_steps,))]
        + [dma((all_steps,))] * 2,
        compiler_params=pltpu.CompilerParams(
            collective_id=0, has_side_effects=True, vmem_limit_bytes=56 << 20
        ),
        name="hyena_fused",
    )(
        query_proj[0],
        key_proj[0],
        value_proj[0],
        out_grad[0],
        offs_ext,
        offs_in,
        valid,
        last,
        passes,
        whole_doc,
        short_taps,
        lam_log,
        coef,
        norm,
        skip_gain[None, :],
    )
    sums = (outs[4], outs[5][0], outs[6])
    if not fused:
        sums = tuple(s * scale for s in lax.psum(sums, ("dp", "ctx")))
    return tuple(o[None] for o in outs[:4]) + sums


def solution(mesh):
    tokens = P("dp", "ctx", None)
    in_specs = (tokens, tokens, tokens, P("dp", "ctx"), P(), P(), P(), P(), tokens)
    out_specs = (tokens, tokens, tokens, tokens, P(), P(), P())
    return jax.shard_map(shards, mesh=mesh, in_specs=in_specs, out_specs=out_specs, check_vma=False)
```

time: 608 us -> 114 us (0.19); the launches traced: 597 us -> 113 us
  other arithmetic: 254 us -> 5.01 us
  waiting for transfers between devices: 160 us -> 0 us
  Pallas kernels: 0 us -> 91.9 us
  local copies, waits for them, and re-layouts: 95.1 us -> 15.1 us
  blocking collectives: 55.6 us -> 0 us
  between operations: 17.1 us -> 1.35 us
  starting transfers between devices: 15.7 us -> 0 us
    psum x1 -> x0, waiting for transfers between devices: 122 us -> none  [shards(): lax.psum((jnp.stack(tap_terms, axis=1), skip_term, residue_term), ('dp',...]
    add x36 -> x0, other arithmetic: 121 us -> none  [the longest x32 79.9 us: advance(): return (term + decay_block * passed[:, None, None] * carried, carried)]
    pallas_call x0 -> x1, Pallas kernels: none -> 91.9 us  [shards(): pl.pallas_call(functools.partial(fused_kernel, (taps, width, dp_count, co...]
    reduce_sum x11 -> x0, other arithmetic: 65.5 us -> none  [the longest x2 19.4 us: shards(): tap_terms.append(jnp.sum(window(tap_index) * short_grads, axis=(1, 2)))]
    psum x1 -> x0, blocking collectives: 36.9 us -> none  [shards(): lax.psum((jnp.stack(tap_terms, axis=1), skip_term, residue_term), ('dp',...]
    dynamic_slice x32 -> x0, local copies, waits for them, and re-layouts: 32.9 us -> none  [sweep(): return lax.scan(advance, initial, (pass_sub.T, terms), reverse=reverse_flag)]
    all_gather x2 -> x0, waiting for transfers between devices: 31.7 us -> none  [the longest x1 31.7 us: shards(): sums = lax.all_gather(block_sum[None], 'ctx', axis=0, tiled=True)]
    dynamic_update_slice x16 -> x0, local copies, waits for them, and re-layouts: 26.8 us -> none  [sweep(): return lax.scan(advance, initial, (pass_sub.T, terms), reverse=reverse_flag)]
  transfers between devices with their start and end apart: 9 -> 0, of which waited for: 5 -> 0; matrix products, arithmetic and copies ran while one was open for 14% -> 0% of each run, Pallas kernels for 0% -> 0%
where the time goes in v2:
time: 114 us; the launch traced here: 113 us
  Pallas kernels  91.9 us (81%)
  local copies, waits for them, and re-layouts  15.1 us (13%)
  other arithmetic  5.01 us (4%)
  between operations  1.35 us (1%)
    pallas_call x1, Pallas kernels, shards(): pl.pallas_call(functools.partial(fused_kernel, (taps, width, dp_count, co...  91.9 us
    unnamed x22, local copies, waits for them, and re-layouts  9.39 us
    broadcast_in_dim x5, local copies, waits for them, and re-layouts, wide(): jnp.broadcast_to(values.astype(F32)[:, None], (values.shape[0], LANES))  3.38 us

profile of v2, /device:TPU:0, one launch (start us, length us, event | category | flops | bytes accessed | tf_op | source)
XLA Modules:
  0.0 113.4 jit_solution(7825212301775032477)
XLA Ops:
  0.6 0.0 copy-start.4
  0.6 1.3 %slice.8 = s32[1,1]{1,0:T(1,128)} slice(s32[1,128]{1,0:T(1,128)} %param.12), slice={[0:1], [127:128]} | slice | bytes 8 | tf_op jit(solution)/shard_map/slice | solution.py:637
  2.6 0.7 compare_convert_fusion.1
  3.2 0.7 fusion
  3.9 0.5 broadcast.77
  4.4 1.3 %fusion.2 = (s32[128]{0:T(128)S(1)}, f32[128]{0:T(128)S(1)}) fusion(s32[1,128]{1,0:T(1,128)} %param.12, s32[]{:T(128)} %broadcast.77), kind=kLoop, calls=%fused_computation.11 | loop fusion | flops 128 | bytes 1540 | tf_op args[3]
  5.7 0.1 pad.6
  5.8 0.6 broadcast_in_dim.65.dev_ref
  6.4 0.1 reshape_squeeze.3
  6.5 0.2 convert_reduce_fusion
  6.7 0.2 subtract_reduce_fusion
  6.9 0.1 broadcast_in_dim.29
  6.9 0.1 sub.17
  7.0 0.7 broadcast_in_dim.64.pass_ref
  7.7 0.7 broadcast_in_dim.30.last_ref
  8.4 0.7 broadcast_in_dim.27.offin_ref
  9.1 0.7 broadcast_in_dim.28.valid_ref
  9.8 0.7 pad.7.offx_ref
  10.5 0.0 copy-done.4
  10.5 2.0 %negate_sqrt_fusion = (f32[16,4096]{1,0:T(8,128)}, f32[16,4096]{1,0:T(8,128)}, f32[16,4096]{1,0:T(8,128)}) fusion(f32[16,4096]{1,0:T(8,128)S(1)} %copy-done.4, f32[16,4096]{1,0:T(8,128)} %param.15), kind=kLoop, calls=%fused_computation | loop fusion | flops 327680 | bytes 1310720 | tf_op jit(solution)/shard_map/sqrt | solution.py:622
  12.6 91.9 %hyena_fused.1 = (bf16[128,4096]{1,0:T(8,128)(2,1)}, bf16[128,4096]{1,0:T(8,128)(2,1)}, bf16[128,4096]{1,0:T(8,128)(2,1)}, bf16[128,4096]{1,0:T(8,128)(2,1)}, f3...) custom-call(bf16[128,4096]{1,0:T(8,128)(2,1)} %bitcast.17, bf16[128,4096]{1,0:T(8,128)(2,1)} %bitcast.18, ...), custom_call_target="tpu_custom_call" | custom-call | tf_op jit(solution)/shard_map/hyena_fused/pallas_call | solution.py:648
  104.5 0.0 copy-start.2
  104.5 2.4 %copy.23 = bf16[1,128,4096]{2,1,0:T(8,128)(2,1)} copy(bf16[1,128,4096]{2,1,0:T(8,128)(2,1)} %bitcast.24) | data formatting | bytes 2097152
  106.9 0.0 copy-done.2
  106.9 0.0 copy-start.1
  106.9 1.0 copy.24
  107.9 0.6 copy-done.1
  108.5 0.0 copy-start
  108.5 1.0 copy.25
  109.5 0.6 copy-done
  110.1 0.0 copy-start.3
  110.1 1.0 copy.26
  111.1 0.3 copy-done.3
  111.3 0.0 copy-start.6
  111.3 0.0 copy-start.5
  111.3 0.7 copy.27
  112.1 0.0 copy-done.6
  112.1 0.6 copy.28
  112.7 0.0 copy-done.5
  112.7 0.7 copy.29
  (1 shorter events, 0.0 us)
Async XLA Ops:
  0.6 9.9 %copy-start.4 = (f32[16,4096]{1,0:T(8,128)S(1)}, f32[16,4096]{1,0:T(8,128)}, u32[]{:S(2)}) copy-start(f32[16,4096]{1,0:T(8,128)} %param.14) | copy-start | bytes 786436
  104.5 2.4 %copy-start.2 = (bf16[128,4096]{1,0:T(8,128)(2,1)S(1)}, bf16[128,4096]{1,0:T(8,128)(2,1)}, u32[]{:S(2)}) copy-start(bf16[128,4096]{1,0:T(8,128)(2,1)} %get-tuple-element.15) | copy-start | bytes 3145732
  106.9 1.6 %copy-start.1 = (bf16[128,4096]{1,0:T(8,128)(2,1)S(1)}, bf16[128,4096]{1,0:T(8,128)(2,1)}, u32[]{:S(2)}) copy-start(bf16[128,4096]{1,0:T(8,128)(2,1)} %get-tuple-element.16) | copy-start | bytes 3145732
  108.5 1.6 %copy-start = (bf16[128,4096]{1,0:T(8,128)(2,1)S(1)}, bf16[128,4096]{1,0:T(8,128)(2,1)}, u32[]{:S(2)}) copy-start(bf16[128,4096]{1,0:T(8,128)(2,1)} %get-tuple-element.17) | copy-start | bytes 3145732
  110.1 1.2 %copy-start.3 = (f32[3,7,4096]{2,1,0:T(8,128)S(1)}, f32[3,7,4096]{2,1,0:T(8,128)}, u32[]{:S(2)}) copy-start(f32[3,7,4096]{2,1,0:T(8,128)} %get-tuple-element.37) | copy-start | bytes 1032196
  111.3 0.8 copy-start.6
  111.3 1.4 %copy-start.5 = (f32[16,4096]{1,0:T(8,128)S(1)}, f32[16,4096]{1,0:T(8,128)}, u32[]{:S(2)}) copy-start(f32[16,4096]{1,0:T(8,128)} %get-tuple-element.39) | copy-start | bytes 786436

commit v3 on v2

--- a/solution.py
+++ b/solution.py
@@ -29,11 +29,6 @@
     v_ref,
     og_ref,
     offx_ref,
-    offin_ref,
-    valid_ref,
-    last_ref,
-    pass_ref,
-    dev_ref,
     short_ref,
     lamlog_ref,
     coef_ref,
@@ -51,6 +46,15 @@
     vs_scr,
     sig_scr,
     gam_scr,
+    offin_ref,
+    valid_ref,
+    last_ref,
+    pass_ref,
+    dev_ref,
+    edge_scr,
+    pack_scr,
+    rim_scr,
+    rim_send,
     rim_recv,
     ends,
     pair_recv,
@@ -92,6 +96,8 @@
     r2,
     s3,
     r3,
+    s4,
+    r4,
 ):
     taps, width, dp_count, count, fused, scale = cfg
     tok, channels = q_ref.shape
@@ -100,7 +106,7 @@
     chunks = channels // width
     tiles = width // LANES
     pairs = count // 2
-    first_main = max(chunks, 2 + 2 * (pairs - 1))
+    first_main = max(chunks, 3 + (5 * (pairs - 1)) // 3)
     me = lax.axis_index("ctx")
     dp = lax.axis_index("dp")
     odd = me % 2
@@ -112,23 +118,31 @@
     sources = (q_ref, k_ref, v_ref)
     rows = lax.broadcasted_iota(jnp.int32, (SUB, LANES), 0).astype(F32)
 
+    rim = taps - 1
+
+    def build_masks(block, carry):
+        at = pl.ds(pl.multiple_of(block * SUB, SUB), SUB)
+        offs = offx_ref[pl.ds(pl.multiple_of(block * SUB + SUB, SUB), SUB), :]
+        end = offx_ref[pl.ds(block * SUB + 2 * SUB - 1, 1), :]
+        offin_ref[at, :] = jnp.minimum(offs, rows)
+        valid_ref[at, :] = jnp.where(offs > rows, 1.0, 0.0)
+        last_ref[at, :] = jnp.where(rows >= float(SUB - 1) - end, 1.0, 0.0)
+        pass_ref[pl.ds(block, 1), :] = jnp.where(end >= float(SUB), 1.0, 0.0)
+        return carry
+
     barrier = pltpu.get_barrier_semaphore()
+    friends = 0
     if fused:
-        others = dp_count * count - 1
-        lin = dp * count + me
-
-        def peer_of(step):
-            peer = (lin + step) % (dp_count * count)
-            return {"dp": peer // count, "ctx": peer % count}
-
-        def greet(step, carry):
-            pl.semaphore_signal(barrier, 1, device_id=peer_of(step), device_id_type=MESH)
-            return carry
-
-        lax.fori_loop(1, others + 1, greet, 0)
-        pl.semaphore_wait(barrier, others)
+        for step in range(1, dp_count):
+            pl.semaphore_signal(
+                barrier, 1, device_id={"dp": (dp + step) % dp_count}, device_id_type=MESH
+            )
+        for step in range(1, count):
+            pl.semaphore_signal(
+                barrier, 1, device_id={"ctx": (me + step) % count}, device_id_type=MESH
+            )
+        friends = dp_count + count - 2
     else:
-        friends = 0
         for hop in (1, -1, 2, -2):
             friend = me + hop
             there = jnp.logical_and(friend >= 0, friend < count)
@@ -140,7 +154,24 @@
                 )
 
             friends = friends + there.astype(jnp.int32)
-        pl.semaphore_wait(barrier, friends)
+    lax.fori_loop(0, blocks, build_masks, 0)
+    dev_ref[...] = jnp.where(
+        jnp.broadcast_to(offx_ref[SUB + tok - 1 : SUB + tok, :], (SUB, LANES)) >= float(tok),
+        1.0,
+        0.0,
+    )
+
+    def pack(chunk, carry):
+        cols = pl.ds(pl.multiple_of(chunk * width, width), width)
+        for branch, ref in enumerate(sources):
+            edge_scr[...] = ref[tok - 2 * SUB : tok, cols].astype(F32)
+            pack_scr[branch * rim : (branch + 1) * rim, :] = edge_scr[2 * SUB - rim :, :]
+        rim_send[chunk] = pack_scr[...].astype(BF16)
+        return carry
+
+    pack_scr[...] = jnp.zeros(pack_scr.shape, F32)
+    lax.fori_loop(0, chunks, pack, 0)
+    pl.semaphore_wait(barrier, friends)
 
     def remote(source, target, send, recv, device):
         return pltpu.make_async_remote_copy(
@@ -161,12 +192,12 @@
     def lane_cols(step):
         return pl.ds(pl.multiple_of(step * LANES, LANES), LANES)
 
-    def rim_copy(chunk, branch):
-        return remote(
-            sources[branch].at[tok - 2 * SUB : tok, chunk_cols(chunk)],
-            rim_recv.at[chunk, branch],
-            rim_s.at[chunk, branch],
-            rim_r.at[chunk, branch],
+    def rim_copy(chunk):
+        return remote(
+            rim_send.at[chunk],
+            rim_recv.at[chunk],
+            rim_s.at[chunk],
+            rim_r.at[chunk],
             {"ctx": me + 1},
         )
 
@@ -221,8 +252,7 @@
     @pl.when(me + 1 < count)
     def _():
         def send(chunk, carry):
-            for branch in range(3):
-                rim_copy(chunk, branch).start()
+            rim_copy(chunk).start()
             return carry
 
         lax.fori_loop(0, chunks, send, 0)
@@ -240,8 +270,10 @@
         chain_recv[1 - odd] = jnp.zeros(chain_recv.shape[1:], F32)
 
     def fill(branch, chunk, step, cols):
-        edge = rim_recv[chunk, branch, :, lane_cols(step)].astype(F32)
-        ext_ref[branch, 0:SUB, :] = edge[SUB:, :]
+        if branch == 0:
+            rim_scr[...] = rim_recv[chunk, :, lane_cols(step)].astype(F32)
+        ext_ref[branch, 0:SUB, :] = jnp.zeros((SUB, LANES), F32)
+        ext_ref[branch, SUB - rim : SUB, :] = rim_scr[branch * rim : (branch + 1) * rim, :]
         source = sources[branch][:, cols].astype(F32)
         ext_ref[branch, SUB:, :] = source
         return source
@@ -428,10 +460,16 @@
             {"dp": peer},
         )
 
+    def owner_of(chunk):
+        return (chunk + count // 2) % count
+
+    my_chunk = (me + count - count // 2) % count
+
     def ctx_copy(chunk):
-        slot = (me - chunk + count) % count - 1
-        return remote(
-            part.at[chunk], ctx_recv.at[slot], s2.at[chunk], r2.at[slot], {"ctx": chunk}
+        owner = owner_of(chunk)
+        slot = (me - owner + count) % count - 1
+        return remote(
+            part.at[chunk], ctx_recv.at[slot], s2.at[chunk], r2.at[slot], {"ctx": owner}
         )
 
     def ctx_arrival(slot):
@@ -439,12 +477,46 @@
             part.at[0], ctx_recv.at[slot], s2.at[0], r2.at[slot], {"ctx": partner}
         )
 
-    mine = tile_cols(me, dp) if fused else None
-
-    def spread_copy(step):
-        return remote(
-            full.at[:, mine], full.at[:, mine], s3.at[step - 1], r3.at[step - 1], peer_of(step)
-        )
+    def gather_copy(chunk, step):
+        place_cols = tile_cols(chunk, dp)
+        return remote(
+            full.at[:, place_cols],
+            full.at[:, place_cols],
+            s3.at[step - 1],
+            r3.at[chunk],
+            {"ctx": (me + step) % count},
+        )
+
+    def forward_copy(chunk, step):
+        place_cols = tile_cols(chunk, dp)
+        return remote(
+            full.at[:, place_cols],
+            full.at[:, place_cols],
+            s4.at[chunk, step - 1],
+            r4.at[chunk, step - 1],
+            {"dp": (dp + step) % dp_count},
+        )
+
+    def forward_arrival(chunk, step):
+        place_cols = tile_cols(chunk, (dp + dp_count - step) % dp_count)
+        return remote(
+            full.at[:, place_cols],
+            full.at[:, place_cols],
+            s4.at[chunk, step - 1],
+            r4.at[chunk, step - 1],
+            {"dp": (dp + step) % dp_count},
+        )
+
+    def sum_parts(done):
+        total = acc[done, :, lane_cols(dp)]
+        for step in range(1, dp_count):
+            dp_copy(done, step).wait_recv()
+            total = total + dp_recv[done, step - 1]
+        part[done] = total
+
+        @pl.when(owner_of(done) != me)
+        def _():
+            ctx_copy(done).start()
 
     flag_copy.wait()
 
@@ -453,13 +525,12 @@
         def _():
             @pl.when(me > 0)
             def _():
-                for branch in range(3):
-                    rim_copy(slot, branch).wait_recv()
+                rim_copy(slot).wait_recv()
 
             each_tile(local_tile, slot)
             pair_copy(slot).start()
 
-        link = slot - 2 - 2 * place
+        link = slot - 3 - (5 * place) // 3
 
         @pl.when(jnp.logical_and(link >= 0, link < chunks))
         def _():
@@ -484,7 +555,17 @@
             def _():
                 cross_arrival(now).wait_recv()
 
-            each_tile(main_tile, now)
+            def one(step, inner):
+                if fused:
+
+                    @pl.when(jnp.logical_and(step == tiles // 2, now > 0))
+                    def _():
+                        sum_parts(now - 1)
+
+                main_tile(now, step)
+                return inner
+
+            lax.fori_loop(0, tiles, one, 0)
 
             @pl.when(me > 0)
             def _():
@@ -499,15 +580,10 @@
         @pl.when(jnp.logical_and(done >= 0, done < chunks))
         def _():
             if fused:
-                total = acc[done, :, lane_cols(dp)]
-                for step in range(1, dp_count):
-                    dp_copy(done, step).wait_recv()
-                    total = total + dp_recv[done, step - 1]
-                part[done] = total
-
-                @pl.when(done != me)
+
+                @pl.when(done == chunks - 1)
                 def _():
-                    ctx_copy(done).start()
+                    sum_parts(chunks - 1)
 
             @pl.when(me + 1 < count)
             def _():
@@ -521,19 +597,26 @@
 
         if fused:
 
-            @pl.when(now - 2 == me)
-            def _():
-                total = part[me]
+            @pl.when(done == my_chunk)
+            def _():
+                total = part[my_chunk]
                 for index in range(count - 1):
                     ctx_arrival(index).wait_recv()
                     total = total + ctx_recv[index]
-                full[:, mine] = total * scale
-
-                def send(step, inner):
-                    spread_copy(step).start()
-                    return inner
-
-                lax.fori_loop(1, others + 1, send, 0)
+                full[:, tile_cols(my_chunk, dp)] = total * scale
+                for step in range(1, count):
+                    gather_copy(my_chunk, step).start()
+
+            ready = now - 2
+
+            @pl.when(jnp.logical_and(ready >= 0, ready < chunks))
+            def _():
+                @pl.when(ready != my_chunk)
+                def _():
+                    gather_copy(ready, 1).wait_recv()
+
+                for step in range(1, dp_count):
+                    forward_copy(ready, step).start()
 
         return carry
 
@@ -541,11 +624,12 @@
 
     if fused:
 
-        def arrive(step, carry):
-            spread_copy(step).wait_recv()
+        def arrive(chunk, carry):
+            for step in range(1, dp_count):
+                forward_arrival(chunk, step).wait_recv()
             return carry
 
-        lax.fori_loop(1, others + 1, arrive, 0)
+        lax.fori_loop(0, chunks, arrive, 0)
 
     def emit(chunk, carry):
         cols = chunk_cols(chunk)
@@ -563,8 +647,7 @@
 
         @pl.when(me + 1 < count)
         def _():
-            for branch in range(3):
-                rim_copy(chunk, branch).wait_send()
+            rim_copy(chunk).wait_send()
 
         @pl.when(place < pairs - 1)
         def _():
@@ -579,7 +662,9 @@
             for step in range(1, dp_count):
                 dp_copy(chunk, step).wait_send()
 
-            @pl.when(chunk != me)
+                forward_copy(chunk, step).wait_send()
+
+            @pl.when(owner_of(chunk) != me)
             def _():
                 ctx_copy(chunk).wait_send()
 
@@ -587,12 +672,35 @@
 
     lax.fori_loop(0, chunks, drain, 0)
     if fused:
-
-        def sent(step, carry):
-            spread_copy(step).wait_send()
-            return carry
-
-        lax.fori_loop(1, others + 1, sent, 0)
+        for step in range(1, count):
+            gather_copy(my_chunk, step).wait_send()
+
+
+def settle_kernel(*refs):
+    half = len(refs) // 2
+    for source, target in zip(refs[:half], refs[half:]):
+        target[...] = source[...]
+
+
+def settle(arrays):
+    channels = arrays[0].shape[-1]
+    width = channels // 4
+
+    def spec(array):
+        zeros = (0,) * (array.ndim - 1)
+        return pl.BlockSpec(array.shape[:-1] + (width,), lambda i: zeros + (i,))
+
+    return pl.pallas_call(
+        settle_kernel,
+        grid=(4,),
+        out_shape=[jax.ShapeDtypeStruct(a.shape, a.dtype) for a in arrays],
+        in_specs=[spec(a) for a in arrays],
+        out_specs=[spec(a) for a in arrays],
+        compiler_params=pltpu.CompilerParams(
+            dimension_semantics=("arbitrary",), vmem_limit_bytes=24 << 20
+        ),
+        name="settle_outputs",
+    )(*arrays)
 
 
 def shards(
@@ -622,25 +730,14 @@
     norm = jnp.sqrt(-jnp.expm1(2.0 * lam_log))
     coef = residue * norm
 
-    offs = doc_offset[0]
-    index = jnp.arange(tok, dtype=jnp.int32) % SUB
-    ends = offs.reshape(blocks, SUB)[:, SUB - 1]
-
-    def wide(values):
-        return jnp.broadcast_to(values.astype(F32)[:, None], (values.shape[0], LANES))
-
-    offs_ext = jnp.pad(wide(offs), ((SUB, SUB), (0, 0)))
-    offs_in = wide(jnp.minimum(offs, index))
-    valid = wide(offs > index)
-    last = wide(index >= SUB - 1 - jnp.repeat(ends, SUB))
-    passes = wide(ends >= SUB)
-    whole_doc = wide(jnp.broadcast_to(offs[tok - 1] >= tok, (SUB,)))
+    offs = jnp.pad(doc_offset[0], (SUB, SUB)).astype(F32)
+    offs_ext = jnp.broadcast_to(offs[:, None], (tok + 2 * SUB, LANES))
 
     acc_rows = -(-(3 * taps + 1) // SUB) * SUB + modes
     dma = pltpu.SemaphoreType.DMA
     vmem = pl.BlockSpec(memory_space=pltpu.VMEM)
     dp_steps, ctx_steps = max(dp_count - 1, 1), max(count - 1, 1)
-    all_steps = dp_count * count - 1 if fused else 1
+    rim_rows = -(-3 * (taps - 1) // (2 * SUB)) * 2 * SUB
 
     def scr(*dims, dtype=F32):
         return pltpu.VMEM(dims, dtype)
@@ -653,12 +750,21 @@
             jax.ShapeDtypeStruct((1, channels), F32),
             jax.ShapeDtypeStruct((modes, channels), F32),
         ],
-        in_specs=[vmem] * 15,
+        in_specs=[vmem] * 10,
         out_specs=[vmem] * 7,
         scratch_shapes=[scr(tok, channels)] * 3
         + [scr(blocks, modes, channels)] * 2
         + [
-            scr(chunks, 3, 2 * SUB, width, dtype=BF16),
+            scr(tok, LANES),
+            scr(tok, LANES),
+            scr(tok, LANES),
+            scr(blocks, LANES),
+            scr(SUB, LANES),
+            scr(2 * SUB, width),
+            scr(rim_rows, width),
+            scr(rim_rows, LANES),
+            scr(chunks, rim_rows, width, dtype=BF16),
+            scr(chunks, rim_rows, width, dtype=BF16),
             scr(2, chunks, modes, width),
             scr(chunks, modes, width),
             scr(chunks, modes, width),
@@ -684,11 +790,11 @@
             dma,
             dma,
         ]
-        + [dma((chunks, 3))] * 2
-        + [dma((chunks,))] * 8
+        + [dma((chunks,))] * 10
         + [dma((chunks, dp_steps))] * 2
         + [dma((chunks,)), dma((ctx_steps,))]
-        + [dma((all_steps,))] * 2,
+        + [dma((ctx_steps,)), dma((chunks,))]
+        + [dma((chunks, dp_steps))] * 2,
         compiler_params=pltpu.CompilerParams(
             collective_id=0, has_side_effects=True, vmem_limit_bytes=56 << 20
         ),
@@ -699,17 +805,13 @@
         value_proj[0],
         out_grad[0],
         offs_ext,
-        offs_in,
-        valid,
-        last,
-        passes,
-        whole_doc,
         short_taps,
         lam_log,
         coef,
         norm,
         skip_gain[None, :],
     )
+    outs = settle(outs)
     sums = (outs[4], outs[5][0], outs[6])
     if not fused:
         sums = tuple(s * scale for s in lax.psum(sums, ("dp", "ctx")))

time: 114 us -> 103 us (0.904)
  local copies, waits for them, and re-layouts: 15.1 us -> 8.92 us
  other arithmetic: 5.01 us -> 2.16 us
  Pallas kernels: 91.9 us -> 90.6 us
    pallas_call x1, Pallas kernels: 91.9 us -> 87.7 us  [shards(): pl.pallas_call(functools.partial(fused_kernel, (taps, width, dp_count, co...]
    pallas_call x0 -> x1, Pallas kernels: none -> 2.92 us  [settle(): pl.pallas_call(settle_kernel, grid=(4,), out_shape=[jax.ShapeDtypeStruct(...]
    broadcast_in_dim x6 -> x1, local copies, waits for them, and re-layouts: 3.45 us -> 0.72 us  [shards(): offs_ext = jnp.broadcast_to(offs[:, None], (tok + 2 * SUB, LANES))]
    unnamed x1 -> x0, other arithmetic: 1.32 us -> none
    slice x1 -> x0, local copies, waits for them, and re-layouts: 1.28 us -> none  [shards(): whole_doc = wide(jnp.broadcast_to(offs[tok - 1] >= tok, (SUB,)))]
    convert_element_type x3 -> x1, other arithmetic: 1.33 us -> 0.07 us  [shards(): offs = jnp.pad(doc_offset[0], (SUB, SUB)).astype(F32)]
    unnamed x22 -> x16, local copies, waits for them, and re-layouts: 9.39 us -> 8.2 us
where the time goes in v3:
time: 103 us; the launch traced here: 102 us
  Pallas kernels  90.6 us (88%)
  local copies, waits for them, and re-layouts  8.92 us (9%)
  other arithmetic  2.16 us (2%)
    pallas_call x1, Pallas kernels, shards(): pl.pallas_call(functools.partial(fused_kernel, (taps, width, dp_count, co...  87.7 us
    unnamed x16, local copies, waits for them, and re-layouts  8.2 us
    pallas_call x1, Pallas kernels, settle(): pl.pallas_call(settle_kernel, grid=(4,), out_shape=[jax.ShapeDtypeStruct(...  2.92 us
    sqrt x1, other arithmetic, shards(): norm = jnp.sqrt(-jnp.expm1(2.0 * lam_log))  2.08 us

profile of v3, /device:TPU:0, one launch (start us, length us, event | category | flops | bytes accessed | tf_op | source)
XLA Modules:
  0.0 102.3 jit_solution(4364113673277031337)
XLA Ops:
  0.6 0.0 copy-start.7
  0.6 0.6 copy-done.7
  1.3 0.1 pad_convert_fusion
  1.4 0.7 broadcast_in_dim.21.offx_ref
  2.1 2.1 %negate_sqrt_fusion = (f32[16,4096]{1,0:T(8,128)}, f32[16,4096]{1,0:T(8,128)}, f32[16,4096]{1,0:T(8,128)}) fusion(f32[16,4096]{1,0:T(8,128)} %param.14, f32[16,4096]{1,0:T(8,128)} %param.15), kind=kLoop, calls=%fused_computation | loop fusion | flops 327680 | bytes 1310720 | tf_op jit(solution)/shard_map/sqrt | solution.py:730
  4.2 87.7 %hyena_fused.1 = (bf16[128,4096]{1,0:T(8,128)(2,1)}, bf16[128,4096]{1,0:T(8,128)(2,1)}, bf16[128,4096]{1,0:T(8,128)(2,1)}, bf16[128,4096]{1,0:T(8,128)(2,1)}, f3...) custom-call(bf16[128,4096]{1,0:T(8,128)(2,1)} %bitcast.11, bf16[128,4096]{1,0:T(8,128)(2,1)} %bitcast.12, ...), custom_call_target="tpu_custom_call" | custom-call | tf_op jit(solution)/shard_map/hyena_fused/pallas_call | solution.py:745
  91.8 0.0 copy-start
  91.9 1.2 %copy-done = bf16[128,4096]{1,0:T(8,128)(2,1)S(1)} copy-done((bf16[128,4096]{1,0:T(8,128)(2,1)S(1)}, bf16[128,4096]{1,0:T(8,128)(2,1)}, u32[]{:S(2)}) %copy-start) | copy-done | bytes 1048600
  93.1 0.0 copy-start.1
  93.1 1.2 %copy-done.1 = bf16[128,4096]{1,0:T(8,128)(2,1)S(1)} copy-done((bf16[128,4096]{1,0:T(8,128)(2,1)S(1)}, bf16[128,4096]{1,0:T(8,128)(2,1)}, u32[]{:S(2)}) %copy-start.1) | copy-done | bytes 1048600
  94.3 0.0 copy-start.2
  94.3 1.2 %copy-done.2 = bf16[128,4096]{1,0:T(8,128)(2,1)S(1)} copy-done((bf16[128,4096]{1,0:T(8,128)(2,1)S(1)}, bf16[128,4096]{1,0:T(8,128)(2,1)}, u32[]{:S(2)}) %copy-start.2) | copy-done | bytes 1048600
  95.5 0.0 copy-start.3
  95.5 1.2 %copy-done.3 = bf16[128,4096]{1,0:T(8,128)(2,1)S(1)} copy-done((bf16[128,4096]{1,0:T(8,128)(2,1)S(1)}, bf16[128,4096]{1,0:T(8,128)(2,1)}, u32[]{:S(2)}) %copy-start.3) | copy-done | bytes 1048600
  96.7 0.0 copy-start.4
  96.7 1.0 copy-done.4
  97.7 0.0 copy-start.5
  97.7 0.9 copy-done.5
  98.7 0.0 copy-start.6
  98.7 0.7 copy-done.6
  99.4 2.9 %settle_outputs.1 = (bf16[128,4096]{1,0:T(8,128)(2,1)}, bf16[128,4096]{1,0:T(8,128)(2,1)}, bf16[128,4096]{1,0:T(8,128)(2,1)}, bf16[128,4096]{1,0:T(8,128)(2,1)},...) custom-call(bf16[128,4096]{1,0:T(8,128)(2,1)S(1)} %copy-done, bf16[128,4096]{1,0:T(8,128)(2,1)S(1)} %copy-done.1, ...), custom_call_target="tpu_custom_call" | custom-call | tf_op jit(solution)/shard_map/settle_outputs/pallas_call | solution.py:693
Async XLA Ops:
  0.6 0.7 copy-start.7
  91.8 1.2 %copy-start = (bf16[128,4096]{1,0:T(8,128)(2,1)S(1)}, bf16[128,4096]{1,0:T(8,128)(2,1)}, u32[]{:S(2)}) copy-start(bf16[128,4096]{1,0:T(8,128)(2,1)} %get-tuple-element.21.refs_0_) | copy-start | bytes 3145732
  93.1 1.2 %copy-start.1 = (bf16[128,4096]{1,0:T(8,128)(2,1)S(1)}, bf16[128,4096]{1,0:T(8,128)(2,1)}, u32[]{:S(2)}) copy-start(bf16[128,4096]{1,0:T(8,128)(2,1)} %get-tuple-element.22.refs_1_) | copy-start | bytes 3145732
  94.3 1.2 %copy-start.2 = (bf16[128,4096]{1,0:T(8,128)(2,1)S(1)}, bf16[128,4096]{1,0:T(8,128)(2,1)}, u32[]{:S(2)}) copy-start(bf16[128,4096]{1,0:T(8,128)(2,1)} %get-tuple-element.23.refs_2_) | copy-start | bytes 3145732
  95.5 1.2 %copy-start.3 = (bf16[128,4096]{1,0:T(8,128)(2,1)S(1)}, bf16[128,4096]{1,0:T(8,128)(2,1)}, u32[]{:S(2)}) copy-start(bf16[128,4096]{1,0:T(8,128)(2,1)} %get-tuple-element.24.refs_3_) | copy-start | bytes 3145732
  96.7 1.0 copy-start.4
  97.7 0.9 copy-start.5
  98.7 0.7 copy-start.6

commit v4 on v3

--- a/solution.py
+++ b/solution.py
@@ -51,6 +51,7 @@
     last_ref,
     pass_ref,
     dev_ref,
+    mask_scr,
     edge_scr,
     pack_scr,
     rim_scr,
@@ -155,6 +156,10 @@
 
             friends = friends + there.astype(jnp.int32)
     lax.fori_loop(0, blocks, build_masks, 0)
+    for tap in range(1, taps):
+        mask_scr[tap - 1] = jnp.where(
+            offx_ref[tap : tap + tok + SUB, :] >= float(tap), 1.0, 0.0
+        )
     dev_ref[...] = jnp.where(
         jnp.broadcast_to(offx_ref[SUB + tok - 1 : SUB + tok, :], (SUB, LANES)) >= float(tok),
         1.0,
@@ -412,7 +417,7 @@
                 tuple(jnp.zeros((SUB, LANES), F32) for _ in range(SUB)),
                 jnp.zeros((modes, LANES), F32),
             ),
-            unroll=2,
+            unroll=4,
         )
         mo_ref[:, cols] = xm_ref[...].astype(BF16)
         res = res * lam
@@ -433,7 +438,7 @@
             for tap in range(taps):
                 moved = g_ref[branch, tap : tap + span_rows, :]
                 if tap > 0:
-                    moved = jnp.where(offx_ref[tap : tap + span_rows, :] >= float(tap), moved, 0.0)
+                    moved = moved * mask_scr[tap - 1]
                 spread = spread + short_ref[branch, tap : tap + 1, cols] * moved
                 row = branch * taps + tap
                 acc[chunk, row : row + 1, at_lanes] = jnp.sum(
@@ -697,7 +702,7 @@
         in_specs=[spec(a) for a in arrays],
         out_specs=[spec(a) for a in arrays],
         compiler_params=pltpu.CompilerParams(
-            dimension_semantics=("arbitrary",), vmem_limit_bytes=24 << 20
+            dimension_semantics=("arbitrary",), vmem_limit_bytes=56 << 20
         ),
         name="settle_outputs",
     )(*arrays)
@@ -760,6 +765,7 @@
             scr(tok, LANES),
             scr(blocks, LANES),
             scr(SUB, LANES),
+            scr(taps - 1, tok + SUB, LANES),
             scr(2 * SUB, width),
             scr(rim_rows, width),
             scr(rim_rows, LANES),

time: 103 us -> 96.4 us (0.936)
  local copies, waits for them, and re-layouts: 8.92 us -> 1.37 us
  Pallas kernels: 90.6 us -> 91.9 us
    unnamed x16 -> x2, local copies, waits for them, and re-layouts: 8.2 us -> 0.65 us
    pallas_call x1, Pallas kernels: 2.92 us -> 5 us  [settle(): pl.pallas_call(settle_kernel, grid=(4,), out_shape=[jax.ShapeDtypeStruct(...]
where the time goes in v4:
time: 96.4 us; the launch traced here: 96.1 us
  Pallas kernels  91.9 us (95%)
  other arithmetic  2.16 us (2%)
  local copies, waits for them, and re-layouts  1.37 us (1%)
    pallas_call x1, Pallas kernels, shards(): pl.pallas_call(functools.partial(fused_kernel, (taps, width, dp_count, co...  86.9 us
    pallas_call x1, Pallas kernels, settle(): pl.pallas_call(settle_kernel, grid=(4,), out_shape=[jax.ShapeDtypeStruct(...  5 us
    sqrt x1, other arithmetic, shards(): norm = jnp.sqrt(-jnp.expm1(2.0 * lam_log))  2.08 us

profile of v4, /device:TPU:0, one launch (start us, length us, event | category | flops | bytes accessed | tf_op | source)
XLA Modules:
  0.0 96.1 jit_solution(3909399250658607917)
XLA Ops:
  0.6 0.0 copy-start
  0.6 0.6 copy-done
  1.3 0.1 pad_convert_fusion
  1.4 0.7 broadcast_in_dim.21.offx_ref
  2.1 2.1 %negate_sqrt_fusion = (f32[16,4096]{1,0:T(8,128)}, f32[16,4096]{1,0:T(8,128)}, f32[16,4096]{1,0:T(8,128)}) fusion(f32[16,4096]{1,0:T(8,128)} %param.14, f32[16,4096]{1,0:T(8,128)} %param.15), kind=kLoop, calls=%fused_computation | loop fusion | flops 327680 | bytes 1310720 | tf_op jit(solution)/shard_map/sqrt | solution.py:735
  4.2 86.9 %hyena_fused.1 = (bf16[128,4096]{1,0:T(8,128)(2,1)}, bf16[128,4096]{1,0:T(8,128)(2,1)}, bf16[128,4096]{1,0:T(8,128)(2,1)}, bf16[128,4096]{1,0:T(8,128)(2,1)}, f3...) custom-call(bf16[128,4096]{1,0:T(8,128)(2,1)} %bitcast.11, bf16[128,4096]{1,0:T(8,128)(2,1)} %bitcast.12, ...), custom_call_target="tpu_custom_call" | custom-call | tf_op jit(solution)/shard_map/hyena_fused/pallas_call | solution.py:750
  91.1 5.0 %settle_outputs.1 = (bf16[128,4096]{1,0:T(8,128)(2,1)}, bf16[128,4096]{1,0:T(8,128)(2,1)}, bf16[128,4096]{1,0:T(8,128)(2,1)}, bf16[128,4096]{1,0:T(8,128)(2,1)},...) custom-call(bf16[128,4096]{1,0:T(8,128)(2,1)} %get-tuple-element.21.refs_0_, ...), custom_call_target="tpu_custom_call" | custom-call | tf_op jit(solution)/shard_map/settle_outputs/pallas_call | solution.py:698
Async XLA Ops:
  0.6 0.7 copy-start

commit v5 on v4

--- a/solution.py
+++ b/solution.py
@@ -318,7 +318,7 @@
 
         zero = jnp.zeros_like(lam)
         total, adjoint, _ = lax.fori_loop(
-            0, blocks, sub_block, (zero, zero, jnp.ones_like(lam)), unroll=4
+            0, blocks, sub_block, (zero, zero, jnp.ones_like(lam)), unroll=8
         )
         ends[1, chunk, :, lane_cols(step)] = total
         ends[0, chunk, :, lane_cols(step)] = adjoint
@@ -363,7 +363,7 @@
             blocks,
             sweep,
             (chain_recv[1, chunk, :, at_lanes], chain_recv[0, chunk, :, at_lanes]),
-            unroll=4,
+            unroll=8,
         )
 
         for branch in range(3):
@@ -417,7 +417,7 @@
                 tuple(jnp.zeros((SUB, LANES), F32) for _ in range(SUB)),
                 jnp.zeros((modes, LANES), F32),
             ),
-            unroll=4,
+            unroll=8,
         )
         mo_ref[:, cols] = xm_ref[...].astype(BF16)
         res = res * lam

time: 96.4 us -> 95.4 us (0.990)
  no operation moved by 1% of the time
where the time goes in v5:
time: 95.4 us; the launch traced here: 95.2 us
  Pallas kernels  91 us (95%)
  other arithmetic  2.16 us (2%)
  local copies, waits for them, and re-layouts  1.37 us (1%)
    pallas_call x1, Pallas kernels, shards(): pl.pallas_call(functools.partial(fused_kernel, (taps, width, dp_count, co...  86 us
    pallas_call x1, Pallas kernels, settle(): pl.pallas_call(settle_kernel, grid=(4,), out_shape=[jax.ShapeDtypeStruct(...  5 us
    sqrt x1, other arithmetic, shards(): norm = jnp.sqrt(-jnp.expm1(2.0 * lam_log))  2.08 us

profile of v5, /device:TPU:0, one launch (start us, length us, event | category | flops | bytes accessed | tf_op | source)
XLA Modules:
  0.0 95.2 jit_solution(5811525730280930891)
XLA Ops:
  0.6 0.0 copy-start
  0.6 0.6 copy-done
  1.3 0.1 pad_convert_fusion
  1.4 0.7 broadcast_in_dim.21.offx_ref
  2.1 2.1 %negate_sqrt_fusion = (f32[16,4096]{1,0:T(8,128)}, f32[16,4096]{1,0:T(8,128)}, f32[16,4096]{1,0:T(8,128)}) fusion(f32[16,4096]{1,0:T(8,128)} %param.14, f32[16,4096]{1,0:T(8,128)} %param.15), kind=kLoop, calls=%fused_computation | loop fusion | flops 327680 | bytes 1310720 | tf_op jit(solution)/shard_map/sqrt | solution.py:735
  4.2 86.0 %hyena_fused.1 = (bf16[128,4096]{1,0:T(8,128)(2,1)}, bf16[128,4096]{1,0:T(8,128)(2,1)}, bf16[128,4096]{1,0:T(8,128)(2,1)}, bf16[128,4096]{1,0:T(8,128)(2,1)}, f3...) custom-call(bf16[128,4096]{1,0:T(8,128)(2,1)} %bitcast.11, bf16[128,4096]{1,0:T(8,128)(2,1)} %bitcast.12, ...), custom_call_target="tpu_custom_call" | custom-call | tf_op jit(solution)/shard_map/hyena_fused/pallas_call | solution.py:750
  90.2 5.0 %settle_outputs.1 = (bf16[128,4096]{1,0:T(8,128)(2,1)}, bf16[128,4096]{1,0:T(8,128)(2,1)}, bf16[128,4096]{1,0:T(8,128)(2,1)}, bf16[128,4096]{1,0:T(8,128)(2,1)},...) custom-call(bf16[128,4096]{1,0:T(8,128)(2,1)} %get-tuple-element.21.refs_0_, ...), custom_call_target="tpu_custom_call" | custom-call | tf_op jit(solution)/shard_map/settle_outputs/pallas_call | solution.py:698
Async XLA Ops:
  0.6 0.7 copy-start
